TPU v7x, 32 devices: a whole 2x2x4 slice. The times are simulated.
32 devices in a mesh: dp: 16 (over z, y, core), tensor: 2 (over x).
Axes of the slice: x: 2, y: 2, z: 4, core: 2. Of those that a mesh axis runs over, the one named last changes fastest.
Arguments:
- tokens: bfloat16 [32, 1024, 768], P('dp', 'tensor'), may hold values from -6 to 6
- segment_ids: int32 [32, 1024], P('dp'), may hold values from 0 to 3, as said below
- timestep: int32 [32], P('dp'), may hold values from 0 to 999
- ln_gain: float32 [768], replicated, may hold values from 0.5 to 1.5
- query_key_value_weight: bfloat16 [3, 768, 768], P(None, None, 'tensor'), may hold values from -0.21875 to 0.21875
- output_projection: bfloat16 [768, 768], P('tensor'), may hold values from -1.75 to 1.75
- up_projection: bfloat16 [768, 3072], P(None, 'tensor'), may hold values from -0.21875 to 0.21875
- down_projection: bfloat16 [3072, 768], P('tensor'), may hold values from -0.109375 to 0.109375
- ada_weight: bfloat16 [128, 2304], replicated, may hold values from -0.5 to 0.5
- ada_bias: float32 [2304], replicated, may hold values from 0.5 to 1.5
- cotangent: bfloat16 [32, 1024, 768], P('dp', 'tensor')
Outputs:
- mixed: bfloat16 [32, 1024, 768], P('dp', 'tensor')
- d_tokens: bfloat16 [32, 1024, 768], P('dp', 'tensor')
- d_ln_gain: float32 [768], replicated
- d_qkv_weight: float32 [3, 768, 768], P(None, None, 'tensor')
- d_out_weight: float32 [768, 768], P('tensor')
- d_up_weight: float32 [768, 3072], P(None, 'tensor')
- d_down_weight: float32 [3072, 768], P('tensor')
- d_ada_weight: float32 [128, 2304], replicated
- d_ada_bias: float32 [2304], replicated
Inputs may be any that keep to these rules, and one draw needn't show every extreme that they name: `segment_ids`: within a sequence the ids never fall and start at 0; equal ids mark one document; the last token has id 3; one document of each sequence covers at least its positions 256 to 767.
All inputs are finite; a program needn't handle non-finite values.
Results may differ from a plain program's by a relative error of at most 0.02.
Values may be sent and summed in bfloat16 or wider, within the bound.
A program may use at most 320 MiB of HBM per device.

v0:
```python
import math

import jax
import jax.numpy as jnp
from jax import lax
from jax.sharding import PartitionSpec as P

HD = 64
TEMB = 128


epsilon = 1e-05
masked_score = -1000000000.0
highest = lax.Precision.HIGHEST


def norm_parts(values):
    centred = values - jnp.mean(values, axis=-1, keepdims=True)
    variance = jnp.mean(centred * centred, axis=-1, keepdims=True)
    inverse = lax.rsqrt(variance + epsilon)
    return (centred * inverse, inverse)


def norm_back(grad_norm, normed, inverse):
    return inverse * (
        grad_norm
        - jnp.mean(grad_norm, axis=-1, keepdims=True)
        - normed * jnp.mean(grad_norm * normed, axis=-1, keepdims=True)
    )


def rotary_tables(length, size):
    half_size = size // 2
    position = jnp.arange(length, dtype=jnp.float32)
    frequency = 10000.0 ** (-jnp.arange(half_size, dtype=jnp.float32) / half_size)
    angles = position[:, None] * frequency[None, :]
    return (jnp.cos(angles)[:, None, :], jnp.sin(angles)[:, None, :])


def rotate(values, cosine, sine):
    half_size = values.shape[-1] // 2
    first_half = values[..., :half_size]
    second_half = values[..., half_size:]
    return jnp.concatenate(
        [first_half * cosine - second_half * sine, second_half * cosine + first_half * sine],
        axis=-1,
    )


def rotate_back(grads, cosine, sine):
    half_size = grads.shape[-1] // 2
    first_half = grads[..., :half_size]
    second_half = grads[..., half_size:]
    return jnp.concatenate(
        [first_half * cosine + second_half * sine, second_half * cosine - first_half * sine],
        axis=-1,
    )


def time_embedding(timestep, width):
    half_size = width // 2
    frequency = jnp.exp(-math.log(10000.0) * jnp.arange(half_size, dtype=jnp.float32) / half_size)
    angles = timestep.astype(jnp.float32)[:, None] * frequency[None, :]
    return jnp.concatenate([jnp.cos(angles), jnp.sin(angles)], axis=-1)


def per_device(
    tokens,
    segment_ids,
    timestep,
    ln_gain,
    query_key_value_weight,
    output_projection,
    up_projection,
    down_projection,
    ada_weight,
    ada_bias,
    cotangent,
):
    batch_size = tokens.shape[0]
    width = tokens.shape[2]
    length = segment_ids.shape[1]
    local_width = output_projection.shape[0]
    heads = local_width // HD
    score_scale = 1.0 / math.sqrt(HD)
    block_rows = min(512, length)
    block_count = length // block_rows

    def split_heads(array):
        return array.reshape(batch_size, length, heads, HD)

    in_float = tokens.astype(jnp.float32)
    normed_one, inverse_one = norm_parts(in_float)
    attn_in = (normed_one * ln_gain).astype(jnp.bfloat16)
    complete_attention_input = lax.all_gather(attn_in, "tensor", axis=1, tiled=True)
    unnormed_rows = jnp.einsum(
        "arb,qbv->qarv",
        complete_attention_input,
        query_key_value_weight,
        preferred_element_type=jnp.float32,
    )
    cosine, sine = rotary_tables(length, HD)
    queries = rotate(split_heads(unnormed_rows[0]), cosine, sine).astype(jnp.bfloat16)
    keys_rot = rotate(split_heads(unnormed_rows[1]), cosine, sine).astype(jnp.bfloat16)
    values_low = split_heads(unnormed_rows[2]).astype(jnp.bfloat16)
    doc_mask = segment_ids[:, :, None] == segment_ids[:, None, :]

    def block_scores(lower):
        scores = (
            jnp.einsum(
                "sqhe,skhe->shqk",
                queries[:, lower : lower + block_rows],
                keys_rot,
                preferred_element_type=jnp.float32,
            )
            * score_scale
        )
        return jnp.where(doc_mask[:, lower : lower + block_rows][:, None], scores, masked_score)

    outputs = []
    log_parts = []
    for block in range(block_count):
        scores = block_scores(block * block_rows)
        largest = jnp.max(scores, axis=-1, keepdims=True)
        exponent = jnp.exp(scores - largest)
        total = jnp.sum(exponent, axis=-1, keepdims=True)
        weights = (exponent / total).astype(jnp.bfloat16)
        outputs.append(
            jnp.einsum("shqk,skhe->sqhe", weights, values_low, preferred_element_type=jnp.float32)
        )
        log_parts.append((largest + jnp.log(total))[..., 0])
    attention_mixture = (
        jnp.concatenate(outputs, axis=1)
        .reshape(batch_size, length, local_width)
        .astype(jnp.bfloat16)
    )
    log_total = jnp.concatenate(log_parts, axis=2)
    attention_share = jnp.einsum(
        "tjk,kr->tjr", attention_mixture, output_projection, preferred_element_type=jnp.float32
    )
    attn_out = lax.psum_scatter(
        attention_share.astype(jnp.bfloat16), "tensor", scatter_dimension=1, tiled=True
    ).astype(jnp.float32)
    hidden = in_float + attn_out
    embedding = time_embedding(timestep, TEMB)
    modulation = jnp.dot(embedding, ada_weight.astype(jnp.float32), precision=highest) + ada_bias
    shift = modulation[:, :width]
    scale = modulation[:, width : 2 * width]
    gate = modulation[:, 2 * width :]
    normed_two, inverse_two = norm_parts(hidden)
    modulated = (normed_two * (1.0 + scale[:, None]) + shift[:, None]).astype(jnp.bfloat16)
    complete_modulated_rows = lax.all_gather(modulated, "tensor", axis=1, tiled=True)
    upward = jnp.einsum(
        "ocp,pj->ocj", complete_modulated_rows, up_projection, preferred_element_type=jnp.float32
    )
    gelu_activation = jax.nn.gelu(upward).astype(jnp.bfloat16)
    branch_part = jnp.einsum(
        "wrp,pi->wri", gelu_activation, down_projection, preferred_element_type=jnp.float32
    )
    branch = lax.psum_scatter(
        branch_part.astype(jnp.bfloat16), "tensor", scatter_dimension=1, tiled=True
    ).astype(jnp.float32)
    mixed = (hidden + gate[:, None] * branch).astype(jnp.bfloat16)
    grad_out = cotangent.astype(jnp.float32)
    grad_gate = jnp.sum(grad_out * branch, axis=1)
    grad_branch = (grad_out * gate[:, None]).astype(jnp.bfloat16)
    complete_branch_gradient = lax.all_gather(grad_branch, "tensor", axis=1, tiled=True)
    grad_down = jnp.einsum(
        "xqi,xqy->iy", gelu_activation, complete_branch_gradient, preferred_element_type=jnp.float32
    )
    grad_activated = jnp.einsum(
        "rvj,ij->rvi", complete_branch_gradient, down_projection, preferred_element_type=jnp.float32
    )
    gelu_pull = jax.vjp(jax.nn.gelu, upward)[1]
    upward_gradient = gelu_pull(grad_activated)[0].astype(jnp.bfloat16)
    grad_up = jnp.einsum(
        "gow,gox->wx", complete_modulated_rows, upward_gradient, preferred_element_type=jnp.float32
    )
    grad_mod_part = jnp.einsum(
        "xhn,bn->xhb", upward_gradient, up_projection, preferred_element_type=jnp.float32
    )
    grad_modulated = lax.psum_scatter(
        grad_mod_part.astype(jnp.bfloat16), "tensor", scatter_dimension=1, tiled=True
    ).astype(jnp.float32)
    grad_shift = jnp.sum(grad_modulated, axis=1)
    grad_scale = jnp.sum(grad_modulated * normed_two, axis=1)
    grad_hidden = grad_out + norm_back(
        grad_modulated * (1.0 + scale[:, None]), normed_two, inverse_two
    )
    grad_modulation = jnp.concatenate([grad_shift, grad_scale, grad_gate], axis=-1)
    grad_ada_weight = jnp.dot(embedding.T, grad_modulation, precision=highest)
    grad_ada_bias = jnp.sum(grad_modulation, axis=0)
    grad_attn_out = grad_hidden.astype(jnp.bfloat16)
    complete_attention_gradient = lax.all_gather(grad_attn_out, "tensor", axis=1, tiled=True)
    grad_out_weight = jnp.einsum(
        "wvt,wvk->tk",
        attention_mixture,
        complete_attention_gradient,
        preferred_element_type=jnp.float32,
    )
    grad_attended = jnp.einsum(
        "pyu,ou->pyo",
        complete_attention_gradient,
        output_projection,
        preferred_element_type=jnp.float32,
    ).astype(jnp.bfloat16)
    grad_heads = split_heads(grad_attended)
    grad_keys = jnp.zeros((batch_size, length, heads, HD), jnp.float32)
    grad_values = jnp.zeros((batch_size, length, heads, HD), jnp.float32)
    grad_query_parts = []
    for block in range(block_count):
        lower = block * block_rows
        query_block = queries[:, lower : lower + block_rows]
        grad_block = grad_heads[:, lower : lower + block_rows]
        probs = jnp.exp(block_scores(lower) - log_total[:, :, lower : lower + block_rows, None])
        grad_values = grad_values + jnp.einsum(
            "shqk,sqhe->skhe",
            probs.astype(jnp.bfloat16),
            grad_block,
            preferred_element_type=jnp.float32,
        )
        grad_probs = jnp.einsum(
            "sqhe,skhe->shqk", grad_block, values_low, preferred_element_type=jnp.float32
        )
        inner = jnp.sum(probs * grad_probs, axis=-1, keepdims=True)
        grad_scores = (probs * (grad_probs - inner)).astype(jnp.bfloat16)
        grad_query_parts.append(
            jnp.einsum("shqk,skhe->sqhe", grad_scores, keys_rot, preferred_element_type=jnp.float32)
            * score_scale
        )
        grad_keys = (
            grad_keys
            + jnp.einsum(
                "shqk,sqhe->skhe", grad_scores, query_block, preferred_element_type=jnp.float32
            )
            * score_scale
        )
    grad_query_raw = rotate_back(jnp.concatenate(grad_query_parts, axis=1), cosine, sine)
    grad_key_raw = rotate_back(grad_keys, cosine, sine)
    unnormed_gradient = (
        jnp.stack([grad_query_raw, grad_key_raw, grad_values])
        .reshape(3, batch_size, length, local_width)
        .astype(jnp.bfloat16)
    )
    grad_qkv = jnp.einsum(
        "ifo,bifg->bog",
        complete_attention_input,
        unnormed_gradient,
        preferred_element_type=jnp.float32,
    )
    grad_in_part = jnp.einsum(
        "tarw,txw->arx",
        unnormed_gradient,
        query_key_value_weight,
        preferred_element_type=jnp.float32,
    )
    grad_normed = lax.psum_scatter(
        grad_in_part.astype(jnp.bfloat16), "tensor", scatter_dimension=1, tiled=True
    ).astype(jnp.float32)
    grad_gain = jnp.sum(grad_normed * normed_one, axis=(0, 1))
    grad_tokens = (grad_hidden + norm_back(grad_normed * ln_gain, normed_one, inverse_one)).astype(
        jnp.bfloat16
    )
    grad_qkv, grad_out_weight, grad_up, grad_down = lax.psum(
        (grad_qkv, grad_out_weight, grad_up, grad_down), "dp"
    )
    grad_gain, grad_ada_weight, grad_ada_bias = lax.psum(
        (grad_gain, grad_ada_weight, grad_ada_bias), ("dp", "tensor")
    )
    return (
        mixed,
        grad_tokens,
        grad_gain,
        grad_qkv,
        grad_out_weight,
        grad_up,
        grad_down,
        grad_ada_weight,
        grad_ada_bias,
    )


def solution(mesh):
    in_specs = (
        P("dp", "tensor", None),
        P("dp", None),
        P("dp"),
        P(),
        P(None, None, "tensor"),
        P("tensor", None),
        P(None, "tensor"),
        P("tensor", None),
        P(),
        P(),
        P("dp", "tensor", None),
    )
    out_specs = (
        P("dp", "tensor", None),
        P("dp", "tensor", None),
        P(),
        P(None, None, "tensor"),
        P("tensor", None),
        P(None, "tensor"),
        P("tensor", None),
        P(),
        P(),
    )
    return jax.shard_map(
        per_device, mesh=mesh, in_specs=in_specs, out_specs=out_specs, check_vma=False
    )
```

profile of v0, /device:TPU:0, one launch (start us, length us, event | category | flops | bytes accessed | tf_op | source)
XLA Modules:
  0.0 1065.2 jit_solution(4879153598707435231)
XLA Ops:
  17.6 43.6 %all-gather.5.cloned.1.call-done = bf16[2,1024,768]{2,1,0:T(8,128)(2,1)} async-done(((bf16[2,512,768]{2,1,0:T(8,128)(2,1)}), bf16[2,1024,768]{2,1,0:T(8,128)(2,1)}) %all-gather.5.cloned.1.call-update) | async-done | bytes 3145744 | tf_op jit(solution)/shard_map/all_gather | solution.py:95
  70.4 10.6 fusion.98
  81.0 10.6 fusion.99
  91.6 11.4 %fusion.1 = f32[2,6,512]{2,1,0:T(8,128)S(1)} fusion(f32[2,6,512,1024]{3,2,1,0:T(8,128)} %get-tuple-element.67, f32[2,6,512]{2,1,0:T(8,128)S(1)} %get-tuple-element.66), kind=kLoop, calls=%fused_computation.13 | loop fusion | flops 12576768 | bytes 25214976 | tf_op jit(solution)/shard_map/reduce_sum | solution.py:126
  103.0 10.4 fusion.73
  113.4 11.0 %fusion = f32[2,6,512]{2,1,0:T(8,128)S(1)} fusion(f32[2,6,512,1024]{3,2,1,0:T(8,128)} %get-tuple-element.69, f32[2,6,512]{2,1,0:T(8,128)S(1)} %get-tuple-element.68), kind=kLoop, calls=%fused_computation.12 | loop fusion | flops 12576768 | bytes 25214976 | tf_op jit(solution)/shard_map/reduce_sum | solution.py:126
  124.4 10.4 fusion.72
  140.6 42.7 %reduce-scatter.5.cloned.1.call-done = bf16[2,512,768]{2,1,0:T(8,128)(2,1)} async-done(((bf16[2,1024,768]{2,1,0:T(8,128)(2,1)}), bf16[2,512,768]{2,1,0:T(8,128)(2,1)}) %reduce-scatter.5.cloned.1.call-update) | async-done | bytes 1572880 | tf_op jit(solution)/shard_map/reduce_scatter | solution.py:141
  191.8 42.1 %all-gather.7.cloned.1.call-done = bf16[2,1024,768]{2,1,0:T(8,128)(2,1)} async-done(((bf16[2,512,768]{2,1,0:T(8,128)(2,1)}), bf16[2,1024,768]{2,1,0:T(8,128)(2,1)}) %all-gather.7.cloned.1.call-update) | async-done | bytes 3145744 | tf_op jit(solution)/shard_map/all_gather | solution.py:152
  234.0 10.0 fusion.54
  244.0 37.0 %all-gather.9.cloned.1.call-done = bf16[2,1024,768]{2,1,0:T(8,128)(2,1)} async-done(((bf16[2,512,768]{2,1,0:T(8,128)(2,1)}), bf16[2,1024,768]{2,1,0:T(8,128)(2,1)}) %all-gather.9.cloned.1.call-update) | async-done | bytes 3145744 | tf_op jit(solution)/shard_map/all_gather | solution.py:167
  281.0 15.6 %fusion.10 = bf16[2,1024,1536]{2,1,0:T(8,128)(2,1)S(1)} fusion(f32[2,1024,1536]{2,1,0:T(8,128)} %fusion.54, bf16[2,1024,768]{2,1,0:T(8,128)(2,1)} %all-gather.9.cloned.1.call-done, bf16[1536,768]{1,0:T(8,128)(2,1)} %param.18), kind=kOutput, calls=%fused_computation.24 | convolution fusion | flops 4894752768 | bytes 24379392 | tf_op jit(solution)/shard_map/rvj,ij->rvi/dot_general | solution.py:171
  305.8 43.4 %reduce-scatter.9.cloned.1.call-done = bf16[2,512,768]{2,1,0:T(8,128)(2,1)} async-done(((bf16[2,1024,768]{2,1,0:T(8,128)(2,1)}), bf16[2,512,768]{2,1,0:T(8,128)(2,1)}) %reduce-scatter.9.cloned.1.call-update) | async-done | bytes 1572880 | tf_op jit(solution)/shard_map/reduce_scatter | solution.py:182
  357.4 44.8 %all-gather.11.cloned.1.call-done = bf16[2,1024,768]{2,1,0:T(8,128)(2,1)} async-done(((bf16[2,512,768]{2,1,0:T(8,128)(2,1)}), bf16[2,1024,768]{2,1,0:T(8,128)(2,1)}) %all-gather.11.cloned.1.call-update) | async-done | bytes 3145744 | tf_op jit(solution)/shard_map/all_gather | solution.py:194
  406.7 12.1 %fusion.11 = f32[2,6,64,1024]{3,2,1,0:T(8,128)} fusion(f32[2,6,512,1024]{3,2,1,0:T(8,128)} %get-tuple-element.67, f32[2,6,512]{2,1,0:T(8,128)S(1)} %log_add_fusion, bf16[2,1024,6,64]{1,3,2,0:T(8,128)(2,1)S(1)} %bitcast.97), kind=kOutput, calls=%fused_computation.25 | convolution fusion | flops 817889280 | bytes 29130752 | tf_op jit(solution)/shard_map/shqk,sqhe->skhe/dot_general | solution.py:216
  418.7 15.8 %multiply_reduce_fusion = (f32[2,6,512]{2,1,0:T(8,128)S(1)}, f32[2,6,512,1024]{3,2,1,0:T(8,128)}) fusion(f32[2,6,512,1024]{3,2,1,0:T(8,128)} %get-tuple-element.67, f32[2,6,512]{2,1,0:T(8,128)S(1)} %log_add_fusion, bf16[2,1024,6,64]{1,3,2,0:T(8,128)(2,1)S(1)} %bitcast.90, bf16[2,1024,6,64]{1,3,2,0:T(8,128)(2,1)} %bitcast.98), kind=kOutput, calls=%fused_computation.1 | convolution fusion | flops 824174592 | bytes 52740096 | tf_op jit(solution)/shard_map/sqhe,skhe->shqk/dot_general | solution.py:222
  434.5 15.8 %multiply_reduce_fusion.1 = (f32[2,6,512]{2,1,0:T(8,128)S(1)}, f32[2,6,512,1024]{3,2,1,0:T(8,128)}) fusion(f32[2,6,512,1024]{3,2,1,0:T(8,128)} %get-tuple-element.69, f32[2,6,512]{2,1,0:T(8,128)S(1)} %log_add_fusion.1, bf16[2,1024,6,64]{1,3,2,0:T(8,128)(2,1)S(1)} %bitcast.91, bf16[2,1024,6,64]{1,3,2,0:T(8,128)(2,1)} %bitcast.99), kind=kOutput, calls=%fused_computation.4 | convolution fusion | flops 824174592 | bytes 52740096 | tf_op jit(solution)/shard_map/sqhe,skhe->shqk/dot_general | solution.py:222
  450.4 22.3 %multiply_convert_fusion.1 = bf16[2,6,512,1024]{3,2,1,0:T(8,128)(2,1)} fusion(f32[2,6,512,1024]{3,2,1,0:T(8,128)} %get-tuple-element.73, f32[2,6,512,1024]{3,2,1,0:T(8,128)} %get-tuple-element.69, f32[2,6,512]{2,1,0:T(8,128)S(1)} %get-tuple-element.72, f32[2,6,512]{2,1,0:T(8,128)S(1)} %log_add_fusion.1), kind=kLoop, calls=%fused_computation.3 | loop fusion | flops 25165824 | bytes 62963712 | tf_op jit(solution)/shard_map/convert_element_type | solution.py:226
  472.7 9.8 multiply_bitcast_fusion.2
  482.5 8.7 fusion.92
  491.1 11.7 %add_convert_fusion = bf16[2,6,64,1024]{3,2,1,0:T(8,128)(2,1)} fusion(f32[2,6,64,1024]{3,2,1,0:T(8,128)S(1)} %copy-done.11, f32[2,6,512,1024]{3,2,1,0:T(8,128)} %get-tuple-element.69, f32[2,6,512]{2,1,0:T(8,128)S(1)} %log_add_fusion.1, bf16[2,1024,6,64]{1,3,2,0:T(8,128)(2,1)S(1)} %bitcast.100), kind=kOutput, calls=%fused_computation.83 | convolution fusion | flops 819462144 | bytes 30703616 | tf_op jit(solution)/shard_map/shqk,sqhe->skhe/dot_general | solution.py:216
  505.4 21.6 %multiply_convert_fusion = bf16[2,6,512,1024]{3,2,1,0:T(8,128)(2,1)} fusion(f32[2,6,512,1024]{3,2,1,0:T(8,128)} %get-tuple-element.71, f32[2,6,512,1024]{3,2,1,0:T(8,128)} %get-tuple-element.67, f32[2,6,512]{2,1,0:T(8,128)S(1)} %get-tuple-element.70, f32[2,6,512]{2,1,0:T(8,128)S(1)} %log_add_fusion), kind=kLoop, calls=%fused_computation | loop fusion | flops 25165824 | bytes 62963712 | tf_op jit(solution)/shard_map/convert_element_type | solution.py:226
  527.0 8.7 multiply_bitcast_fusion.1
  547.4 8.9 bitcast_convert_fusion
  557.9 11.5 %fusion.59 = bf16[2,1024,768]{2,1,0:T(8,128)(2,1)} fusion(bf16[1536,768]{1,0:T(8,128)(2,1)S(1)} %copy-done.66, f32[2,1024,1536]{2,1,0:T(8,128)} %fusion.54), kind=kOutput, calls=%fused_computation.97 | convolution fusion | flops 4861722624 | bytes 18087936 | tf_op jit(solution)/shard_map/wrp,pi->wri/dot_general | solution.py:157
  569.5 10.0 convolution_bitcast_fusion.1
  579.5 11.1 %convolution_bitcast_fusion = f32[1536,768]{1,0:T(8,128)} fusion(bf16[2,1024,768]{2,1,0:T(8,128)(2,1)S(1)} %copy-done.64, f32[2,1024,1536]{2,1,0:T(8,128)} %fusion.54), kind=kOutput, calls=%fused_computation.53 | convolution fusion | flops 4860149760 | bytes 20447232 | tf_op jit(solution)/shard_map/xqi,xqy->iy/dot_general | solution.py:168
  603.6 41.8 %reduce-scatter.7.cloned.1.call-done = bf16[2,512,768]{2,1,0:T(8,128)(2,1)} async-done(((bf16[2,1024,768]{2,1,0:T(8,128)(2,1)}), bf16[2,512,768]{2,1,0:T(8,128)(2,1)}) %reduce-scatter.7.cloned.1.call-update) | async-done | bytes 1572880 | tf_op jit(solution)/shard_map/reduce_scatter | solution.py:160
  645.5 7.3 fusion.33
  655.1 41.4 %all-reduce = (f32[768]{0:T(1024)}, f32[2304]{0:T(1024)}) all-reduce(f32[768]{0:T(1024)S(1)} %get-tuple-element.29, f32[2304]{0:T(1024)S(1)} %fusion.91), channel_id=1, replica_groups=mesh['dp'=16,'tensor'=2] {'dp','tensor'}, use_global_device_ids=true, to_apply=%region_19.20 | all-reduce | flops 3072 | bytes 24576 | tf_op jit(solution)/shard_map/psum | solution.py:267
  696.5 213.8 %all-reduce.7.cloned.1.call-done = (f32[3,768,384]{1,2,0:T(8,128)}, f32[384,768]{1,0:T(8,128)}, f32[768,1536]{1,0:T(8,128)}, f32[1536,768]{1,0:T(8,128)}) async-done(((f32[3,768,384]{1,2,0:T(8,128)}, f32[384,768]{1,0:T(8,128)}, f32[768,1536]{1,0:T(8,128)}, f32[1536,768]{1,0:T(8,128)}), (f32[3,768,384]{1,2,0:T(8,128)}, f32[384,768]{1,0:T(8,128)}, f32[768,1536]{1,0:T(8,128)}, ...) | async-done | bytes 14155792 | tf_op jit(solution)/shard_map/psum | solution.py:264
  915.6 131.7 %all-reduce.5.cloned.1.call-done = f32[128,2304]{1,0:T(8,128)} async-done(((f32[128,2304]{1,0:T(8,128)}), f32[128,2304]{1,0:T(8,128)}) %all-reduce.5.cloned.1.call-update) | async-done | bytes 1179664 | tf_op jit(solution)/shard_map/psum | solution.py:267
  (220 shorter events, 102.3 us)
Async XLA Ops:
  7.2 226.8 %copy-start = (bf16[768,1536]{1,0:T(8,128)(2,1)S(1)}, bf16[768,1536]{1,0:T(8,128)(2,1)}, u32[]{:S(2)}) copy-start(bf16[768,1536]{1,0:T(8,128)(2,1)} %param.17) | copy-start | bytes 7077892
  7.2 54.0 %all-gather.5.cloned.1.call-start = ((), (), s32[]{:S(2)}) async-start(), calls=%async_computation.4 | async-start | bytes 4718592 | tf_op jit(solution)/shard_map/all_gather | solution.py:95
  13.5 169.8 %reduce-scatter.5.cloned.1.call-start = ((), (), s32[]{:S(2)}) async-start(), calls=%async_computation.5 | async-start | bytes 4718592 | tf_op jit(solution)/shard_map/reduce_scatter | solution.py:141
  14.1 55.0 %copy-start.28 = (f32[1024,32]{0,1:T(8,128)}, f32[1024,32]{0,1:T(8,128)S(1)}, u32[]{:S(2)}) copy-start(f32[1024,32]{0,1:T(8,128)S(1)} %get-tuple-element.64) | copy-start | bytes 393220
  14.1 55.0 %copy-start.30 = (f32[1024,32]{0,1:T(8,128)}, f32[1024,32]{0,1:T(8,128)S(1)}, u32[]{:S(2)}) copy-start(f32[1024,32]{0,1:T(8,128)S(1)} %get-tuple-element.65) | copy-start | bytes 393220
  68.0 56.4 %copy-start.8 = (bf16[1,2,1024,384]{2,3,0,1:T(8,128)(2,1)}, bf16[1,2,1024,384]{2,3,0,1:T(8,128)(2,1)S(1)}, u32[]{:S(2)}) copy-start(bf16[1,2,1024,384]{2,3,0,1:T(8,128)(2,1)S(1)} %slice.153) | copy-start | bytes 4718596
  139.7 94.2 %all-gather.7.cloned.1.call-start = ((), (), s32[]{:S(2)}) async-start(), calls=%async_computation.6 | async-start | bytes 4718592 | tf_op jit(solution)/shard_map/all_gather | solution.py:152
  140.5 48.4 %copy-start.49 = (f32[2,768]{1,0:T(2,128)}, f32[2,768]{1,0:T(2,128)S(1)}, u32[]{:S(2)}) copy-start(f32[2,768]{1,0:T(2,128)S(1)} %get-tuple-element.59) | copy-start | bytes 18436
  140.5 212.6 %copy-start.37 = (f32[2,768]{1,0:T(2,128)}, f32[2,768]{1,0:T(2,128)S(1)}, u32[]{:S(2)}) copy-start(f32[2,768]{1,0:T(2,128)S(1)} %get-tuple-element.61) | copy-start | bytes 18436
  186.1 167.1 %copy-start.39 = (f32[2,512]{1,0:T(2,128)}, f32[2,512]{1,0:T(2,128)S(1)}, u32[]{:S(2)}) copy-start(f32[2,512]{1,0:T(2,128)S(1)} %broadcast_multiply_fusion.4) | copy-start | bytes 12292
  186.9 166.3 %copy-start.43 = (f32[2,512]{1,0:T(2,128)}, f32[2,512]{1,0:T(2,128)S(1)}, u32[]{:S(2)}) copy-start(f32[2,512]{1,0:T(2,128)S(1)} %add_rsqrt_fusion) | copy-start | bytes 12292
  188.9 92.1 %all-gather.9.cloned.1.call-start = ((), (), s32[]{:S(2)}) async-start(), calls=%async_computation.8 | async-start | bytes 4718592 | tf_op jit(solution)/shard_map/all_gather | solution.py:167
  191.8 157.5 %reduce-scatter.9.cloned.1.call-start = ((), (), s32[]{:S(2)}) async-start(), calls=%async_computation.9 | async-start | bytes 4718592 | tf_op jit(solution)/shard_map/reduce_scatter | solution.py:182
  305.7 43.5 %copy-start.4 = (bf16[2,512,768]{2,1,0:T(8,128)(2,1)S(1)}, bf16[2,512,768]{2,1,0:T(8,128)(2,1)}, u32[]{:S(2)}) copy-start(bf16[2,512,768]{2,1,0:T(8,128)(2,1)} %param.11) | copy-start | bytes 4718596
  305.8 96.4 %all-gather.11.cloned.1.call-start = ((), (), s32[]{:S(2)}) async-start(), calls=%async_computation.10 | async-start | bytes 4718592 | tf_op jit(solution)/shard_map/all_gather | solution.py:194
  353.2 49.0 %copy-start.68 = (bf16[384,768]{1,0:T(8,128)(2,1)S(1)}, bf16[384,768]{1,0:T(8,128)(2,1)}, u32[]{:S(2)}) copy-start(bf16[384,768]{1,0:T(8,128)(2,1)} %param.16) | copy-start | bytes 1769476
  357.1 242.6 %reduce-scatter.11.cloned.1.call-start = ((), (), s32[]{:S(2)}) async-start(), calls=%async_computation.11 | async-start | bytes 4718592 | tf_op jit(solution)/shard_map/reduce_scatter | solution.py:257
  450.4 22.3 %copy-start.19 = (bf16[2,1024,6,32]{1,3,2,0:T(8,128)(2,1)S(1)}, bf16[2,1024,6,32]{1,3,2,0:T(8,128)(2,1)}, u32[]{:S(2)}) copy-start(bf16[2,1024,6,32]{1,3,2,0:T(8,128)(2,1)} %copy-done.18) | copy-start | bytes 2359300
  556.2 89.2 %reduce-scatter.7.cloned.1.call-start = ((), (), s32[]{:S(2)}) async-start(), calls=%async_computation.7 | async-start | bytes 4718592 | tf_op jit(solution)/shard_map/reduce_scatter | solution.py:160
  569.4 340.9 %all-reduce.7.cloned.1.call-start = ((), (), s32[]{:S(2)}) async-start(), calls=%async_computation.13 | async-start | bytes 28311552 | tf_op jit(solution)/shard_map/psum | solution.py:264
  599.1 46.4 %copy-start.38 = (f32[2,768]{1,0:T(2,128)S(1)}, f32[2,768]{1,0:T(2,128)}, u32[]{:S(2)}) copy-start(f32[2,768]{1,0:T(2,128)} %copy-done.37) | copy-start | bytes 18436
  599.1 46.4 %copy-start.40 = (f32[2,512]{1,0:T(2,128)S(1)}, f32[2,512]{1,0:T(2,128)}, u32[]{:S(2)}) copy-start(f32[2,512]{1,0:T(2,128)} %copy-done.39) | copy-start | bytes 12292
  599.1 46.4 %copy-start.44 = (f32[2,512]{1,0:T(2,128)S(1)}, f32[2,512]{1,0:T(2,128)}, u32[]{:S(2)}) copy-start(f32[2,512]{1,0:T(2,128)} %copy-done.43) | copy-start | bytes 12292
  599.1 46.4 %copy-start.50 = (f32[2,768]{1,0:T(2,128)S(1)}, f32[2,768]{1,0:T(2,128)}, u32[]{:S(2)}) copy-start(f32[2,768]{1,0:T(2,128)} %copy-done.49) | copy-start | bytes 18436
  599.1 46.4 %copy-start.54 = (f32[2,512]{1,0:T(2,128)S(1)}, f32[2,512]{1,0:T(2,128)}, u32[]{:S(2)}) copy-start(f32[2,512]{1,0:T(2,128)} %copy-done.53) | copy-start | bytes 12292
  599.1 46.4 %copy-start.56 = (f32[2,512]{1,0:T(2,128)S(1)}, f32[2,512]{1,0:T(2,128)}, u32[]{:S(2)}) copy-start(f32[2,512]{1,0:T(2,128)} %copy-done.55) | copy-start | bytes 12292
  599.1 448.1 %all-reduce.5.cloned.1.call-start = ((), (), s32[]{:S(2)}) async-start(), calls=%async_computation.12 | async-start | bytes 2359296 | tf_op jit(solution)/shard_map/psum | solution.py:267
  603.6 49.2 %copy-start.47 = (f32[2,768]{1,0:T(2,128)S(1)}, f32[2,768]{1,0:T(2,128)}, u32[]{:S(2)}) copy-start(f32[2,768]{1,0:T(2,128)} %get-tuple-element.27) | copy-start | bytes 18436
  603.6 49.2 %copy-start.48 = (f32[2,768]{1,0:T(2,128)S(1)}, f32[2,768]{1,0:T(2,128)}, u32[]{:S(2)}) copy-start(f32[2,768]{1,0:T(2,128)} %get-tuple-element.33) | copy-start | bytes 18436
  603.6 49.2 %copy-start.60 = (f32[2,64]{1,0:T(2,128)S(1)}, f32[2,64]{1,0:T(2,128)}, u32[]{:S(2)}) copy-start(f32[2,64]{1,0:T(2,128)} %copy-done.59) | copy-start | bytes 1540
  603.6 49.2 %copy-start.62 = (f32[2,64]{1,0:T(2,128)S(1)}, f32[2,64]{1,0:T(2,128)}, u32[]{:S(2)}) copy-start(f32[2,64]{1,0:T(2,128)} %copy-done.61) | copy-start | bytes 1540
  910.3 136.9 %copy-start.32 = (f32[384,768]{1,0:T(8,128)S(1)}, f32[384,768]{1,0:T(8,128)}, u32[]{:S(2)}) copy-start(f32[384,768]{1,0:T(8,128)} %get-tuple-element.80) | copy-start | bytes 3538948
  (51 other events, 288.3 us)
Sparse Core Ops, SparseCore 0:
  13.6 47.6 all-gather.4
  139.9 43.3 reduce-scatter.4
  189.0 44.9 all-gather.6
  236.0 44.9 all-gather.8
  305.9 43.3 reduce-scatter.8
  357.2 44.9 all-gather.10
  556.4 43.3 reduce-scatter.10
  602.1 43.3 reduce-scatter.6
  650.6 259.6 all-reduce.6
  916.2 131.0 all-reduce.4
where the time goes:
time: 1080 us; the launch traced here: 1070 us
  waiting for transfers between devices  641 us (59%)
  matrix products  229 us (21%)
  other arithmetic  103 us (10%)
  blocking collectives  41.4 us (4%)
  local copies, waits for them, and re-layouts  34 us (3%)
  between operations  15.5 us (1%)
    psum x1, waiting for transfers between devices, per_device(): lax.psum((grad_qkv, grad_out_weight, grad_up, grad_down), 'dp')  214 us
    psum x1, waiting for transfers between devices, per_device(): lax.psum((grad_gain, grad_ada_weight, grad_ada_bias), ('dp', 'tensor'))  132 us
    all_gather x1, waiting for transfers between devices, per_device(): lax.all_gather(grad_attn_out, 'tensor', axis=1, tiled=True)  44.8 us
    convert_element_type x2, other arithmetic, per_device(): grad_scores = (probs * (grad_probs - inner)).astype(jnp.bfloat16)  43.8 us
    all_gather x1, waiting for transfers between devices, per_device(): lax.all_gather(attn_in, 'tensor', axis=1, tiled=True)  43.6 us
    reduce_scatter x1, waiting for transfers between devices, per_device(): lax.psum_scatter(grad_mod_part.astype(jnp.bfloat16), 'tensor', scatter_di...  43.4 us
    reduce_scatter x1, waiting for transfers between devices, per_device(): lax.psum_scatter(attention_share.astype(jnp.bfloat16), 'tensor', scatter_...  42.7 us
    all_gather x1, waiting for transfers between devices, per_device(): lax.all_gather(modulated, 'tensor', axis=1, tiled=True)  42.1 us
  transfers between devices with their start and end apart: 10, of which 10 were waited for; matrix products, arithmetic and copies ran while one was open for 7% of the time, Pallas kernels for 0%

commit v1 on v0

v1 whole, which is shorter than its diff:
```python
import functools
import math

import jax
import jax.numpy as jnp
import numpy as np
from jax import lax
from jax.experimental import pallas as pl
from jax.experimental.pallas import tpu as pltpu
from jax.sharding import PartitionSpec as P

HD = 64
TEMB = 128
EPS = 1e-05
MASKED = -1000000000.0
f32 = jnp.float32
bf16 = jnp.bfloat16
VMEM_LIMIT = 56 * 1024 * 1024


def dot_nn(a, b):
    return lax.dot_general(a, b, (((1,), (0,)), ((), ())), preferred_element_type=f32)


def dot_nt(a, b):
    return lax.dot_general(a, b, (((1,), (1,)), ((), ())), preferred_element_type=f32)


def dot_tn(a, b):
    return lax.dot_general(a, b, (((0,), (0,)), ((), ())), preferred_element_type=f32)


def norm_parts(values):
    centred = values - jnp.mean(values, axis=-1, keepdims=True)
    variance = jnp.mean(centred * centred, axis=-1, keepdims=True)
    inverse = lax.rsqrt(variance + EPS)
    return centred * inverse, inverse


def norm_back(grad, normed, inverse):
    return inverse * (
        grad
        - jnp.mean(grad, axis=-1, keepdims=True)
        - normed * jnp.mean(grad * normed, axis=-1, keepdims=True)
    )


def rotary_np(length):
    half = HD // 2
    position = np.arange(length, dtype=np.float32)
    frequency = (10000.0 ** (-np.arange(half, dtype=np.float32) / half)).astype(np.float32)
    angles = position[:, None] * frequency[None, :]
    cosine, sine = np.cos(angles), np.sin(angles)
    cosine = np.concatenate([cosine, cosine] * 2, axis=1).astype(np.float32)
    sine = np.concatenate([-sine, sine] * 2, axis=1).astype(np.float32)
    return cosine, sine


def swap_halves(values):
    lane = lax.broadcasted_iota(jnp.int32, values.shape, 1)
    first = (lane % HD) < (HD // 2)
    return jnp.where(first, pltpu.roll(values, 128 - HD // 2, 1), pltpu.roll(values, HD // 2, 1))


def params(**kw):
    return pltpu.CompilerParams(vmem_limit_bytes=VMEM_LIMIT, **kw)


def cost(flops, nbytes, trans=0):
    return pl.CostEstimate(flops=int(flops), bytes_accessed=int(nbytes), transcendentals=int(trans))


def qkv_kernel(x_ref, gain_ref, w_ref, cos_ref, sin_ref, n_ref, q_ref, k_ref, v_ref):
    normed, _ = norm_parts(x_ref[...].astype(f32))
    normed = (normed * gain_ref[...]).astype(bf16)
    n_ref[...] = normed
    cosine, sine = cos_ref[...], sin_ref[...]
    width = q_ref.shape[1]
    for which, out in ((0, q_ref), (1, k_ref)):
        raw = dot_nn(normed, w_ref[which])
        for pair in range(width // 128):
            part = raw[:, pair * 128 : pair * 128 + 128]
            turned = (part * cosine + swap_halves(part) * sine).astype(bf16)
            if which == 0:
                turned = turned * jnp.asarray(0.125, bf16)
            out[:, pair * 128 : pair * 128 + 128] = turned
    v_ref[...] = dot_nn(normed, w_ref[2]).astype(bf16)


def qkv_call(x, gain, w, cosine, sine):
    length, width = x.shape
    out = w.shape[2]
    rows = 256
    row = lambda n: pl.BlockSpec((rows, n), lambda i: (i, 0))
    return pl.pallas_call(
        qkv_kernel,
        grid=(length // rows,),
        in_specs=[
            row(width),
            pl.BlockSpec((1, width), lambda i: (0, 0)),
            pl.BlockSpec((3, width, out), lambda i: (0, 0, 0)),
            row(128),
            row(128),
        ],
        out_specs=[row(width), row(out), row(out), row(out)],
        out_shape=[jax.ShapeDtypeStruct((length, width), bf16)]
        + [jax.ShapeDtypeStruct((length, out), bf16)] * 3,
        compiler_params=params(),
        cost_estimate=cost(2 * length * width * 3 * out, 2 * length * width + 6 * width * out),
    )(x, gain, w, cosine, sine)


def attend_kernel(q_ref, k_ref, v_ref, segc_ref, segr_ref, o_ref, lse_ref):
    rows = q_ref.shape[0]
    lane = lax.broadcasted_iota(jnp.int32, (1, 128), 1)
    q, k, v = q_ref[...], k_ref[...], v_ref[...]
    mask = segc_ref[...] == segr_ref[...]
    low = lane < HD
    parts = []
    for head in range(2):
        mine = low if head == 0 else jnp.logical_not(low)
        scores = dot_nt(jnp.where(mine, q, jnp.zeros_like(q)), k)
        scores = jnp.where(mask, scores, MASKED)
        largest = jnp.max(scores, axis=1, keepdims=True)
        weights = jnp.exp(scores - largest).astype(bf16)
        mixed = dot_nn(weights, jnp.where(mine, v, jnp.ones_like(v)))
        total = pltpu.roll(mixed, HD, 1)
        parts.append((mixed / total, largest + jnp.log(total)))
    o_ref[...] = jnp.where(low, parts[0][0], parts[1][0]).astype(bf16)
    lse = jnp.where(low, parts[0][1], parts[1][1]).T
    lse_ref[0, 0:1, :] = lse[0:1, :]
    lse_ref[0, 1:2, :] = lse[HD : HD + 1, :]


def attend_call(q, k, v, segc, segr):
    length, width = q.shape
    pairs = width // 128
    rows = 256
    return pl.pallas_call(
        attend_kernel,
        grid=(pairs, length // rows),
        in_specs=[
            pl.BlockSpec((rows, 128), lambda p, i: (i, p)),
            pl.BlockSpec((length, 128), lambda p, i: (0, p)),
            pl.BlockSpec((length, 128), lambda p, i: (0, p)),
            pl.BlockSpec((rows, 1), lambda p, i: (i, 0)),
            pl.BlockSpec((1, length), lambda p, i: (0, 0)),
        ],
        out_specs=[
            pl.BlockSpec((rows, 128), lambda p, i: (i, p)),
            pl.BlockSpec((1, 8, rows), lambda p, i: (p, 0, i)),
        ],
        out_shape=[
            jax.ShapeDtypeStruct((length, width), bf16),
            jax.ShapeDtypeStruct((pairs, 8, length), f32),
        ],
        compiler_params=params(),
        cost_estimate=cost(
            4 * 4 * length * length * width, 8 * length * width, length * length * width // HD
        ),
    )(q, k, v, segc, segr)


def attend_back_kernel(
    q_ref, k_ref, v_ref, o_ref, do_ref, lse_ref, segc_ref, segr_ref, cos_ref, sin_ref,
    dq_ref, dk_ref, dv_ref, acc_ref,
):
    length = q_ref.shape[0]
    rows = 256
    lane = lax.broadcasted_iota(jnp.int32, (1, 128), 1)
    low = lane < HD
    q, do = q_ref[...], do_ref[...]
    product = do.astype(f32) * o_ref[...].astype(f32)
    high_part = product.astype(bf16)
    low_part = (product - high_part.astype(f32)).astype(bf16)
    row8 = lax.broadcasted_iota(jnp.int32, (8, 128), 0)
    lane8 = lax.broadcasted_iota(jnp.int32, (8, 128), 1)
    select = jnp.where((lane8 // HD) == row8, 1.0, 0.0).astype(bf16)
    delta = dot_nt(select, high_part) + dot_nt(select, low_part)
    lse = lse_ref[0]
    segr = segr_ref[...]
    zero = jnp.zeros_like(q)
    q_heads = (jnp.where(low, q, zero), jnp.where(low, zero, q))
    do_heads = (jnp.where(low, do, zero), jnp.where(low, zero, do))
    acc_ref[...] = jnp.zeros_like(acc_ref)
    for block in range(length // rows):
        span = pl.ds(block * rows, rows)
        k, v = k_ref[span, :], v_ref[span, :]
        mask = segc_ref[span, :] == segr
        dv = jnp.zeros((rows, 128), f32)
        dk = jnp.zeros((rows, 128), f32)
        dq = jnp.zeros((128, length), f32)
        for head in range(2):
            mine = low if head == 0 else jnp.logical_not(low)
            kh = jnp.where(mine, k, jnp.zeros_like(k))
            vh = jnp.where(mine, v, jnp.zeros_like(v))
            scores = jnp.where(mask, dot_nt(kh, q), MASKED)
            probs = jnp.exp(scores - lse[head : head + 1, :])
            dv = dv + dot_nn(probs.astype(bf16), do_heads[head])
            d_probs = dot_nt(vh, do)
            d_scores = (probs * (d_probs - delta[head : head + 1, :])).astype(bf16)
            dk = dk + dot_nn(d_scores, q_heads[head])
            dq = dq + dot_tn(kh, d_scores)
        acc_ref[...] += dq
        cosine, sine = cos_ref[span, :], sin_ref[span, :]
        dk_ref[span, :] = (dk * cosine - swap_halves(dk) * sine).astype(bf16)
        dv_ref[span, :] = dv.astype(bf16)
    dq = acc_ref[...].T * 0.125
    dq_ref[...] = (dq * cos_ref[...] - swap_halves(dq) * sin_ref[...]).astype(bf16)


def attend_back_call(q, k, v, o, do, lse, segc, segr, cosine, sine):
    length, width = q.shape
    pairs = width // 128
    whole = pl.BlockSpec((length, 128), lambda p: (0, p))
    fixed = pl.BlockSpec((length, 128), lambda p: (0, 0))
    return pl.pallas_call(
        attend_back_kernel,
        grid=(pairs,),
        in_specs=[whole] * 5
        + [
            pl.BlockSpec((1, 8, length), lambda p: (p, 0, 0)),
            pl.BlockSpec((length, 1), lambda p: (0, 0)),
            pl.BlockSpec((1, length), lambda p: (0, 0)),
            fixed,
            fixed,
        ],
        out_specs=[whole] * 3,
        out_shape=[jax.ShapeDtypeStruct((length, width), bf16)] * 3,
        scratch_shapes=[pltpu.VMEM((128, length), f32)],
        compiler_params=params(),
        cost_estimate=cost(
            10 * 4 * length * length * width, 16 * length * width, length * length * width // HD
        ),
    )(q, k, v, o, do, lse, segc, segr, cosine, sine)


def middle_kernel(
    x_ref, cot_ref, oa_ref, ob_ref, wa_ref, wb_ref, mod_ref, hidden_ref, modul_ref, dbranch_ref
):
    hidden = x_ref[...].astype(f32) + (
        dot_nn(oa_ref[...], wa_ref[...]) + dot_nn(ob_ref[...], wb_ref[...])
    )
    hidden_ref[...] = hidden
    normed, _ = norm_parts(hidden)
    shift, scale, gate = mod_ref[0:1, :], mod_ref[1:2, :], mod_ref[2:3, :]
    modul_ref[...] = (normed * (1.0 + scale) + shift).astype(bf16)
    dbranch_ref[...] = (cot_ref[...].astype(f32) * gate).astype(bf16)


def middle_call(x, cot, oa, ob, wa, wb, mod):
    length, width = x.shape
    rows = 256
    row = lambda n: pl.BlockSpec((rows, n), lambda i: (i, 0))
    full = lambda a: pl.BlockSpec(a.shape, lambda i: (0, 0))
    return pl.pallas_call(
        middle_kernel,
        grid=(length // rows,),
        in_specs=[row(width), row(width), row(oa.shape[1]), row(ob.shape[1]), full(wa), full(wb), full(mod)],
        out_specs=[row(width)] * 3,
        out_shape=[
            jax.ShapeDtypeStruct((length, width), f32),
            jax.ShapeDtypeStruct((length, width), bf16),
            jax.ShapeDtypeStruct((length, width), bf16),
        ],
        compiler_params=params(),
        cost_estimate=cost(2 * length * width * width, 14 * length * width),
    )(x, cot, oa, ob, wa, wb, mod)


def gelu_both(u):
    c0 = math.sqrt(2.0 / math.pi)
    square = u * u
    t = jnp.tanh(u * (c0 + (c0 * 0.044715) * square))
    half = 0.5 + 0.5 * t
    act = u * half
    slope = half + (0.5 * u) * (1.0 - t * t) * (c0 + (3.0 * c0 * 0.044715) * square)
    return act, slope


def feed_kernel(
    modul_ref, dbranch_ref, up_ref, down_ref, bin_ref, din_ref,
    branch_ref, dmod_ref, dup_ref, ddown_ref, act_scr, dupw_scr,
):
    step = pl.program_id(0)

    @pl.when(step == 0)
    def _():
        branch_ref[...] = bin_ref[...]
        dmod_ref[...] = din_ref[...]

    length = modul_ref.shape[0]
    rows = 256
    for block in range(length // rows):
        span = pl.ds(block * rows, rows)
        u = dot_nn(modul_ref[span, :], up_ref[...])
        act, slope = gelu_both(u)
        act = act.astype(bf16)
        act_scr[span, :] = act
        d_act = dot_nt(dbranch_ref[span, :], down_ref[...])
        d_up = (d_act * slope).astype(bf16)
        dupw_scr[span, :] = d_up
        branch_ref[span, :] += dot_nn(act, down_ref[...])
        dmod_ref[span, :] += dot_nt(d_up, up_ref[...])
    dup_ref[...] = dot_tn(modul_ref[...], dupw_scr[...]).astype(bf16)
    ddown_ref[...] = dot_tn(act_scr[...], dbranch_ref[...]).astype(bf16)


def feed_call(modul, dbranch, up, down, branch_in, dmod_in):
    length, width = modul.shape
    hidden = up.shape[1]
    block = 512
    full = pl.BlockSpec((length, width), lambda j: (0, 0))
    return pl.pallas_call(
        feed_kernel,
        grid=(hidden // block,),
        in_specs=[
            full,
            full,
            pl.BlockSpec((width, block), lambda j: (0, j)),
            pl.BlockSpec((block, width), lambda j: (j, 0)),
            full,
            full,
        ],
        out_specs=[
            full,
            full,
            pl.BlockSpec((width, block), lambda j: (0, j)),
            pl.BlockSpec((block, width), lambda j: (j, 0)),
        ],
        out_shape=[
            jax.ShapeDtypeStruct((length, width), f32),
            jax.ShapeDtypeStruct((length, width), f32),
            jax.ShapeDtypeStruct((width, hidden), bf16),
            jax.ShapeDtypeStruct((hidden, width), bf16),
        ],
        scratch_shapes=[pltpu.VMEM((length, block), bf16), pltpu.VMEM((length, block), bf16)],
        compiler_params=params(),
        cost_estimate=cost(12 * length * width * hidden, 16 * length * width + 8 * width * hidden),
    )(modul, dbranch, up, down, branch_in, dmod_in)


def between_kernel(
    hidden_ref, cot_ref, branch_ref, dmod_ref, mod_ref, oa_ref, ob_ref, wa_ref, wb_ref,
    mixed_ref, dhidden_ref, doa_ref, dob_ref, dwa_ref, dwb_ref, sums_ref, dattn_scr,
):
    length = hidden_ref.shape[0]
    rows = 256
    scale, gate = mod_ref[1:2, :], mod_ref[2:3, :]
    sums_ref[...] = jnp.zeros_like(sums_ref)
    for block in range(length // rows):
        span = pl.ds(block * rows, rows)
        hidden = hidden_ref[span, :]
        dout = cot_ref[span, :].astype(f32)
        branch = branch_ref[span, :]
        mixed_ref[span, :] = (hidden + gate * branch).astype(bf16)
        normed, inverse = norm_parts(hidden)
        dmod = dmod_ref[span, :]
        sums_ref[0:1, :] += jnp.sum(dmod, axis=0, keepdims=True)
        sums_ref[1:2, :] += jnp.sum(dmod * normed, axis=0, keepdims=True)
        sums_ref[2:3, :] += jnp.sum(dout * branch, axis=0, keepdims=True)
        dhidden = dout + norm_back(dmod * (1.0 + scale), normed, inverse)
        dhidden_ref[span, :] = dhidden
        dattn = dhidden.astype(bf16)
        dattn_scr[span, :] = dattn
        doa_ref[span, :] = dot_nt(dattn, wa_ref[...]).astype(bf16)
        dob_ref[span, :] = dot_nt(dattn, wb_ref[...]).astype(bf16)
    dwa_ref[...] = dot_tn(oa_ref[...], dattn_scr[...]).astype(bf16)
    dwb_ref[...] = dot_tn(ob_ref[...], dattn_scr[...]).astype(bf16)


def between_call(hidden, cot, branch, dmod, mod, oa, ob, wa, wb):
    length, width = hidden.shape
    spec = pl.BlockSpec(memory_space=pltpu.VMEM)
    half = oa.shape[1]
    return pl.pallas_call(
        between_kernel,
        in_specs=[spec] * 9,
        out_specs=[spec] * 7,
        out_shape=[
            jax.ShapeDtypeStruct((length, width), bf16),
            jax.ShapeDtypeStruct((length, width), f32),
            jax.ShapeDtypeStruct((length, half), bf16),
            jax.ShapeDtypeStruct((length, half), bf16),
            jax.ShapeDtypeStruct((half, width), bf16),
            jax.ShapeDtypeStruct((half, width), bf16),
            jax.ShapeDtypeStruct((8, width), f32),
        ],
        scratch_shapes=[pltpu.VMEM((length, width), bf16)],
        compiler_params=params(),
        cost_estimate=cost(4 * length * width * width, 24 * length * width),
    )(hidden, cot, branch, dmod, mod, oa, ob, wa, wb)


def last_kernel(
    x_ref, n_ref, gain_ref, dhidden_ref,
    dqa_ref, dka_ref, dva_ref, dqb_ref, dkb_ref, dvb_ref, wa_ref, wb_ref,
    dtok_ref, dgain_ref, dwa_ref, dwb_ref,
):
    length = x_ref.shape[0]
    rows = 256
    dgain_ref[...] = jnp.zeros_like(dgain_ref)
    sides = (((dqa_ref, dka_ref, dva_ref), wa_ref, dwa_ref), ((dqb_ref, dkb_ref, dvb_ref), wb_ref, dwb_ref))
    for block in range(length // rows):
        span = pl.ds(block * rows, rows)
        dnormed = jnp.zeros((rows, x_ref.shape[1]), f32)
        for grads, w_ref, _ in sides:
            for which in range(3):
                dnormed = dnormed + dot_nt(grads[which][span, :], w_ref[which])
        normed, inverse = norm_parts(x_ref[span, :].astype(f32))
        dgain_ref[0:1, :] += jnp.sum(dnormed * normed, axis=0, keepdims=True)
        dtok_ref[span, :] = (
            dhidden_ref[span, :] + norm_back(dnormed * gain_ref[...], normed, inverse)
        ).astype(bf16)
    for grads, _, dw_ref in sides:
        for which in range(3):
            dw_ref[which] = dot_tn(n_ref[...], grads[which][...]).astype(bf16)


def last_call(x, n, gain, dhidden, grads_a, grads_b, wa, wb):
    length, width = x.shape
    spec = pl.BlockSpec(memory_space=pltpu.VMEM)
    return pl.pallas_call(
        last_kernel,
        in_specs=[spec] * 12,
        out_specs=[spec] * 4,
        out_shape=[
            jax.ShapeDtypeStruct((length, width), bf16),
            jax.ShapeDtypeStruct((8, width), f32),
            jax.ShapeDtypeStruct(wa.shape, bf16),
            jax.ShapeDtypeStruct(wb.shape, bf16),
        ],
        compiler_params=params(),
        cost_estimate=cost(12 * length * width * width, 30 * length * width),
    )(x, n, gain, dhidden, *grads_a, *grads_b, wa, wb)


def time_embedding(timestep):
    half = TEMB // 2
    frequency = jnp.exp(-math.log(10000.0) * jnp.arange(half, dtype=f32) / half)
    angles = timestep.astype(f32)[:, None] * frequency[None, :]
    return jnp.concatenate([jnp.cos(angles), jnp.sin(angles)], axis=-1)


SWAP = ((0, 1), (1, 0))


def per_device(
    tokens, segment_ids, timestep, ln_gain, w_qkv, w_out, w_up, w_down, ada_weight, ada_bias, cotangent
):
    half, width = tokens.shape[1], tokens.shape[2]
    length = 2 * half
    side = lax.axis_index("tensor")
    pick = lambda a, i: lax.dynamic_index_in_dim(a, i, 0, keepdims=False)

    def swap(a):
        return lax.ppermute(a, "tensor", SWAP)

    def whole_sequence(a):
        mine, came = pick(a, side), swap(pick(a, 1 - side))
        first = jnp.where(side == 0, mine, came)
        second = jnp.where(side == 0, came, mine)
        return jnp.concatenate([first, second], axis=0)

    def split_sequence(a):
        halves = a.reshape(2, half, width)
        came = swap(pick(halves, 1 - side))
        mine = pick(halves, side)
        first = jnp.where(side == 0, mine, came)
        second = jnp.where(side == 0, came, mine)
        return jnp.stack([first, second])

    x = whole_sequence(tokens)
    cot = whole_sequence(cotangent)
    o_qkv, o_out, o_up, o_down = swap(w_qkv), swap(w_out), swap(w_up), swap(w_down)
    segments = pick(segment_ids, side)
    segc, segr = segments.reshape(length, 1), segments.reshape(1, length)
    gain = ln_gain.reshape(1, width)
    cosine, sine = (jnp.asarray(a) for a in rotary_np(length))

    embedding = time_embedding(timestep)
    mine = pick(embedding, side)
    mod = jnp.sum(mine[:, None] * ada_weight.astype(f32), axis=0) + ada_bias
    mod = mod.reshape(3, width)

    n, qa, ka, va = qkv_call(x, gain, w_qkv, cosine, sine)
    oa, lsea = attend_call(qa, ka, va, segc, segr)
    _, qb, kb, vb = qkv_call(x, gain, o_qkv, cosine, sine)
    ob, lseb = attend_call(qb, kb, vb, segc, segr)
    hidden, modul, dbranch = middle_call(x, cot, oa, ob, w_out, o_out, mod)
    zero = jnp.zeros((length, width), f32)
    branch, dmod, dup_a, ddown_a = feed_call(modul, dbranch, w_up, w_down, zero, zero)
    branch, dmod, dup_b, ddown_b = feed_call(modul, dbranch, o_up, o_down, branch, dmod)
    mixed, dhidden, doa, dob, dwo_a, dwo_b, sums = between_call(
        hidden, cot, branch, dmod, mod, oa, ob, w_out, o_out
    )
    grads_a = attend_back_call(qa, ka, va, oa, doa, lsea, segc, segr, cosine, sine)
    grads_b = attend_back_call(qb, kb, vb, ob, dob, lseb, segc, segr, cosine, sine)
    dtok, dgain, dwq_a, dwq_b = last_call(x, n, gain, dhidden, grads_a, grads_b, w_qkv, o_qkv)

    def total(own, other):
        return lax.psum(own + swap(other), "dp").astype(f32)

    d_qkv = total(dwq_a, dwq_b)
    d_out = total(dwo_a, dwo_b)
    d_up = total(dup_a, dup_b)
    d_down = total(ddown_a, ddown_b)

    small = jnp.concatenate([sums[:3].reshape(3 * width), dgain[0], mine])
    every = lax.all_gather(small, ("dp", "tensor"), axis=0)
    d_mods = every[:, : 3 * width]
    d_gain = jnp.sum(every[:, 3 * width : 4 * width], axis=0)
    d_ada_weight = jnp.dot(every[:, 4 * width :].T, d_mods, precision=lax.Precision.HIGHEST)
    d_ada_bias = jnp.sum(d_mods, axis=0)
    return (
        split_sequence(mixed),
        split_sequence(dtok),
        d_gain,
        d_qkv,
        d_out,
        d_up,
        d_down,
        d_ada_weight,
        d_ada_bias,
    )


def solution(mesh):
    in_specs = (
        P("dp", "tensor", None),
        P("dp", None),
        P("dp"),
        P(),
        P(None, None, "tensor"),
        P("tensor", None),
        P(None, "tensor"),
        P("tensor", None),
        P(),
        P(),
        P("dp", "tensor", None),
    )
    out_specs = (
        P("dp", "tensor", None),
        P("dp", "tensor", None),
        P(),
        P(None, None, "tensor"),
        P("tensor", None),
        P(None, "tensor"),
        P("tensor", None),
        P(),
        P(),
    )
    return jax.shard_map(
        per_device, mesh=mesh, in_specs=in_specs, out_specs=out_specs, check_vma=False
    )
```

time: 1080 us -> 563 us (0.52)
  waiting for transfers between devices: 641 us -> 226 us
  matrix products: 229 us -> 2.14 us
  Pallas kernels: 0 us -> 173 us
  other arithmetic: 103 us -> 29.1 us
  blocking collectives: 41.4 us -> 80.5 us
  local copies, waits for them, and re-layouts: 34 us -> 12.5 us
  starting transfers between devices: 0.88 us -> 15.8 us
    psum x2 -> x1, waiting for transfers between devices: 345 us -> 52.4 us  [total(): return lax.psum(own + swap(other), 'dp').astype(f32)]
    dot_general x26 -> x1, matrix products: 229 us -> 2.14 us  [per_device(): jnp.dot(every[:, 4 * width:].T, d_mods, precision=lax.Precision.HIGHEST)]
    ppermute x0 -> x12, waiting for transfers between devices: none -> 174 us  [swap(): return lax.ppermute(a, 'tensor', SWAP)]
    pallas_call x0 -> x11, Pallas kernels: none -> 173 us  [the longest x2 45.5 us: feed_call(): pl.pallas_call(feed_kernel, grid=(hidden // block,), in_specs=[full, full...]
    all_gather x4 -> x0, waiting for transfers between devices: 167 us -> none  [the longest x1 44.8 us: per_device(): lax.all_gather(grad_attn_out, 'tensor', axis=1, tiled=True)]
    reduce_scatter x4 -> x0, waiting for transfers between devices: 128 us -> none  [the longest x1 43.4 us: per_device(): lax.psum_scatter(grad_mod_part.astype(jnp.bfloat16), 'tensor', scatter_di...]
    all_gather x0 -> x1, blocking collectives: none -> 80.5 us  [per_device(): every = lax.all_gather(small, ('dp', 'tensor'), axis=0)]
    convert_element_type x8 -> x5, other arithmetic: 61.5 us -> 10.8 us  [the longest x4 9.68 us: total(): return lax.psum(own + swap(other), 'dp').astype(f32)]
  transfers between devices with their start and end apart: 10 -> 13, of which waited for: 10 -> 6; matrix products, arithmetic and copies ran while one was open for 7% -> 5% of each run, Pallas kernels for 0% -> 27%
where the time goes in v1:
time: 563 us; the launch traced here: 554 us
  waiting for transfers between devices  226 us (40%)
  Pallas kernels  173 us (31%)
  blocking collectives  80.5 us (14%)
  other arithmetic  29.1 us (5%)
  starting transfers between devices  15.8 us (3%)
  between operations  14.7 us (3%)
  local copies, waits for them, and re-layouts  12.5 us (2%)
    ppermute x12, waiting for transfers between devices, swap(): return lax.ppermute(a, 'tensor', SWAP)  174 us
    all_gather x1, blocking collectives, per_device(): every = lax.all_gather(small, ('dp', 'tensor'), axis=0)  80.5 us
    psum x1, waiting for transfers between devices, total(): return lax.psum(own + swap(other), 'dp').astype(f32)  52.4 us
    pallas_call x2, Pallas kernels, feed_call(): pl.pallas_call(feed_kernel, grid=(hidden // block,), in_specs=[full, full...  45.5 us
    pallas_call x2, Pallas kernels, attend_back_call(): pl.pallas_call(attend_back_kernel, grid=(pairs,), in_specs=[whole] * 5 +...  42.2 us
    pallas_call x2, Pallas kernels, attend_call(): pl.pallas_call(attend_kernel, grid=(pairs, length // rows), in_specs=[pl....  36.5 us
    pallas_call x1, Pallas kernels, last_call(): pl.pallas_call(last_kernel, in_specs=[spec] * 12, out_specs=[spec] * 4, o...  17.3 us
    ppermute x12, starting transfers between devices, swap(): return lax.ppermute(a, 'tensor', SWAP)  15.8 us
  transfers between devices with their start and end apart: 13, of which 6 were waited for; matrix products, arithmetic and copies ran while one was open for 5% of the time, Pallas kernels for 27%

profile of v1, /device:TPU:0, one launch (start us, length us, event | category | flops | bytes accessed | tf_op | source)
XLA Modules:
  0.0 554.0 jit_solution(7160481897622745517)
XLA Ops:
  7.2 3.0 collective-permute-start.3
  12.6 1.9 collective-permute-start
  14.6 1.9 collective-permute-start.4
  23.0 35.4 %collective-permute-done = bf16[512,768]{1,0:T(8,128)(2,1)} collective-permute-done((bf16[512,768]{1,0:T(8,128)(2,1)}, bf16[512,768]{1,0:T(8,128)(2,1)}, u32[]{:S(2)}, u32[]{:S(2)}) %collective-permute-start) | collective-permute-done | bytes 786464 | tf_op jit(solution)/shard_map/ppermute | solution.py:457
  58.4 2.1 collective-permute-start.5
  63.1 7.1 %shard_map.196 = (bf16[1024,768]{1,0:T(8,128)(2,1)}, bf16[1024,384]{1,0:T(8,128)(2,1)}, bf16[1024,384]{1,0:T(8,128)(2,1)}, bf16[1024,384]{1,0:T(8,128)(2,1)}) custom-call(bf16[1024,768]{1,0:T(8,128)(2,1)} %pad_maximum_fusion.x_ref, f32[1,768]{1,0:T(1,128)} %reshape.46.gain_ref, bf16[3,768,384]{2,1,0:T(8,128)(2,1)} %wa_ref.5, ...), custom_call_target="tpu_custom_call" | custom-call | flops 1811939328 | bytes 3342336 | tf_op jit(solution)/shard_map/pallas_call | solution.py:95
  71.5 18.3 %shard_map.197 = (bf16[1024,384]{1,0:T(8,128)(2,1)}, f32[3,8,1024]{2,1,0:T(8,128)}) custom-call(bf16[1024,384]{1,0:T(8,128)(2,1)} %get-tuple-element.48.q_ref, bf16[1024,384]{1,0:T(8,128)(2,1)} %get-tuple-element.49.k_ref, bf16[1024,384]{1,0:T(8,128)(2,1)} %get-tuple-element.50.v_ref, s32[1024,1]{1,0:T(8,128)} %copy.26.segc_ref, ...), custom_call_target="tpu_custom_call" | custom-call | flops 6442450944 | bytes 3145728 | tf_op jit(solution)/shard_map/pallas_call | solution.py:139
  91.0 5.3 collective-permute-done.2.w_ref.wb_ref
  96.4 7.0 %shard_map.198 = (bf16[1024,768]{1,0:T(8,128)(2,1)}, bf16[1024,384]{1,0:T(8,128)(2,1)}, bf16[1024,384]{1,0:T(8,128)(2,1)}, bf16[1024,384]{1,0:T(8,128)(2,1)}) custom-call(bf16[1024,768]{1,0:T(8,128)(2,1)} %pad_maximum_fusion.x_ref, f32[1,768]{1,0:T(1,128)} %reshape.46.gain_ref, bf16[3,768,384]{2,1,0:T(8,128)(2,1)} %collective-permute-done.2.w_ref.wb_ref, ...), custom_call_target="tpu_custom_call" | custom-call | flops 1811939328 | bytes 3342336 | tf_op jit(solution)/shard_map/pallas_call | solution.py:95
  103.4 18.2 %shard_map.199 = (bf16[1024,384]{1,0:T(8,128)(2,1)}, f32[3,8,1024]{2,1,0:T(8,128)}) custom-call(bf16[1024,384]{1,0:T(8,128)(2,1)} %get-tuple-element.52.q_ref, bf16[1024,384]{1,0:T(8,128)(2,1)} %get-tuple-element.53.k_ref, bf16[1024,384]{1,0:T(8,128)(2,1)} %get-tuple-element.54.v_ref, s32[1024,1]{1,0:T(8,128)} %copy.26.segc_ref, ...), custom_call_target="tpu_custom_call" | custom-call | flops 6442450944 | bytes 3145728 | tf_op jit(solution)/shard_map/pallas_call | solution.py:139
  122.4 6.9 %shard_map.200 = (f32[1024,768]{1,0:T(8,128)}, bf16[1024,768]{1,0:T(8,128)(2,1)}, bf16[1024,768]{1,0:T(8,128)(2,1)}) custom-call(bf16[1024,768]{1,0:T(8,128)(2,1)} %pad_maximum_fusion.x_ref, bf16[1024,768]{1,0:T(8,128)(2,1)} %pad_maximum_fusion.1.cot_ref, bf16[1024,384]{1,0:T(8,128)(2,1)} %get-tuple-element.51.oa_ref.o_ref, ...), custom_call_target="tpu_custom_call" | custom-call | flops 1207959552 | bytes 11010048 | tf_op jit(solution)/shard_map/pallas_call | solution.py:256
  129.3 1.9 broadcast_in_dim.2.bin_ref.din_ref
  131.2 22.8 %shard_map.201 = (f32[1024,768]{1,0:T(8,128)}, f32[1024,768]{1,0:T(8,128)}, bf16[768,1536]{1,0:T(8,128)(2,1)}, bf16[1536,768]{1,0:T(8,128)(2,1)}) custom-call(bf16[1024,768]{1,0:T(8,128)(2,1)} %get-tuple-element.57.modul_ref, bf16[1024,768]{1,0:T(8,128)(2,1)} %get-tuple-element.58.dbranch_ref, bf16[768,1536]{1,0:T(8,128)(2,1)} %up_ref.1, ...), custom_call_target="tpu_custom_call" | custom-call | flops 14495514624 | bytes 22020096 | tf_op jit(solution)/shard_map/pallas_call | solution.py:314
  154.0 42.6 %collective-permute-done.5.down_ref = bf16[1536,768]{1,0:T(8,128)(2,1)S(1)} collective-permute-done((bf16[1536,768]{1,0:T(8,128)(2,1)}, bf16[1536,768]{1,0:T(8,128)(2,1)S(1)}, u32[]{:S(2)}, u32[]{:S(2)}) %collective-permute-start.5) | collective-permute-done | bytes 2359328 | tf_op jit(solution)/shard_map/ppermute | solution.py:457
  197.9 22.7 %shard_map.202 = (f32[1024,768]{1,0:T(8,128)}, f32[1024,768]{1,0:T(8,128)}, bf16[768,1536]{1,0:T(8,128)(2,1)}, bf16[1536,768]{1,0:T(8,128)(2,1)}) custom-call(bf16[1024,768]{1,0:T(8,128)(2,1)} %get-tuple-element.57.modul_ref, bf16[1024,768]{1,0:T(8,128)(2,1)} %get-tuple-element.58.dbranch_ref, bf16[768,1536]{1,0:T(8,128)(2,1)} %collective-permute-done.4.up_ref, ...), custom_call_target="tpu_custom_call" | custom-call | flops 14495514624 | bytes 22020096 | tf_op jit(solution)/shard_map/pallas_call | solution.py:314
  220.6 1.7 collective-permute-start.10
  222.6 10.8 %shard_map.203 = (bf16[1024,768]{1,0:T(8,128)(2,1)}, f32[1024,768]{1,0:T(8,128)}, bf16[1024,384]{1,0:T(8,128)(2,1)}, bf16[1024,384]{1,0:T(8,128)(2,1)}, bf16[384...) custom-call(f32[1024,768]{1,0:T(8,128)} %get-tuple-element.56.hidden_ref, ...), custom_call_target="tpu_custom_call" | custom-call | flops 2415919104 | bytes 18874368 | tf_op jit(solution)/shard_map/pallas_call | solution.py:376
  233.4 21.1 %shard_map.205 = (bf16[1024,384]{1,0:T(8,128)(2,1)}, bf16[1024,384]{1,0:T(8,128)(2,1)}, bf16[1024,384]{1,0:T(8,128)(2,1)}) custom-call(bf16[1024,384]{1,0:T(8,128)(2,1)} %get-tuple-element.52.q_ref, bf16[1024,384]{1,0:T(8,128)(2,1)} %get-tuple-element.53.k_ref, bf16[1024,384]{1,0:T(8,128)(2,1)} %get-tuple-element.54.v_ref, ...), custom_call_target="tpu_custom_call" | custom-call | flops 16106127360 | bytes 6291456 | tf_op jit(solution)/shard_map/pallas_call | solution.py:217
  254.5 21.1 %shard_map.204 = (bf16[1024,384]{1,0:T(8,128)(2,1)}, bf16[1024,384]{1,0:T(8,128)(2,1)}, bf16[1024,384]{1,0:T(8,128)(2,1)}) custom-call(bf16[1024,384]{1,0:T(8,128)(2,1)} %get-tuple-element.48.q_ref, bf16[1024,384]{1,0:T(8,128)(2,1)} %get-tuple-element.49.k_ref, bf16[1024,384]{1,0:T(8,128)(2,1)} %get-tuple-element.50.v_ref, ...), custom_call_target="tpu_custom_call" | custom-call | flops 16106127360 | bytes 6291456 | tf_op jit(solution)/shard_map/pallas_call | solution.py:217
  275.6 17.3 %shard_map.206 = (bf16[1024,768]{1,0:T(8,128)(2,1)}, f32[8,768]{1,0:T(8,128)}, bf16[3,768,384]{2,1,0:T(8,128)(2,1)}, bf16[3,768,384]{2,1,0:T(8,128)(2,1)}) custom-call(bf16[1024,768]{1,0:T(8,128)(2,1)} %pad_maximum_fusion.x_ref, bf16[1024,768]{1,0:T(8,128)(2,1)} %get-tuple-element.64.n_ref, f32[1,768]{1,0:T(1,128)} %reshape.46.gain_ref, ...), custom_call_target="tpu_custom_call" | custom-call | flops 7247757312 | bytes 23592960 | tf_op jit(solution)/shard_map/pallas_call | solution.py:423
  293.0 1.7 collective-permute-start.8
  295.0 79.4 %collective-permute-done.9 = bf16[384,768]{1,0:T(8,128)(2,1)S(1)} collective-permute-done((bf16[384,768]{1,0:T(8,128)(2,1)S(1)}, bf16[384,768]{1,0:T(8,128)(2,1)S(1)}, u32[]{:S(2)}, u32[]{:S(2)}) %collective-permute-start.9) | collective-permute-done | bytes 589856 | tf_op jit(solution)/shard_map/ppermute | solution.py:457
  377.6 2.1 add.46
  379.7 2.0 add.47
  385.1 80.5 %all-gather.1 = f32[32,1,3200]{2,1,0:T(1,128)S(1)} all-gather(f32[1,1,3200]{2,1,0:T(1,128)S(1)} %reshape.53), channel_id=2, replica_groups=mesh['dp'=16,'tensor'=2] {'dp','tensor'}, dimensions={0}, use_global_device_ids=true | all-gather | bytes 422400 | tf_op jit(solution)/shard_map/all_gather | solution.py:510
  468.0 2.1 fusion.4
  471.6 10.8 %collective-permute-done.7 = bf16[512,768]{1,0:T(8,128)(2,1)S(1)} collective-permute-done((bf16[512,768]{1,0:T(8,128)(2,1)S(1)}, bf16[512,768]{1,0:T(8,128)(2,1)S(1)}, u32[]{:S(2)}, u32[]{:S(2)}) %collective-permute-start.7) | collective-permute-done | bytes 786464 | tf_op jit(solution)/shard_map/ppermute | solution.py:457
  483.8 52.4 %all-reduce.3.cloned.1.call-done = (bf16[3,768,384]{2,1,0:T(8,128)(2,1)}, bf16[384,768]{1,0:T(8,128)(2,1)}, bf16[768,1536]{1,0:T(8,128)(2,1)}, bf16[1536,768]{1,0:T(8,128)(2,1)}) async-done(((bf16[3,768,384]{2,1,0:T(8,128)(2,1)}, bf16[384,768]{1,0:T(8,128)(2,1)}, bf16[768,1536]{1,0:T(8,128)(2,1)}, bf16[1536,768]{1,0:T(8,128)(2,1)}), (bf16[3,768,384]{2,1,0:T(8,128)(2,1)}, bf16[384,768]{1,0:T(8,128)(2,1)}, ...) | async-done | bytes 7077904 | tf_op jit(solution)/shard_map/psum | solution.py:502
  536.2 2.3 convert_element_type.21
  538.5 2.0 convert_element_type.20
  541.3 2.8 convert_element_type.22
  544.1 2.5 convert_element_type.23
  (87 shorter events, 29.4 us)
Async XLA Ops:
  7.2 12.2 %copy-start = (s32[2,1024]{1,0:T(2,128)S(1)}, s32[2,1024]{1,0:T(2,128)}, u32[]{:S(2)}) copy-start(s32[2,1024]{1,0:T(2,128)} %param.14) | copy-start | bytes 24580
  7.2 4.5 copy-start.9
  7.2 529.0 %all-reduce.3.cloned.1.call-start = ((), (), s32[]{:S(2)}) async-start(), calls=%async_computation | async-start | bytes 14155776 | tf_op jit(solution)/shard_map/psum | solution.py:502
  7.2 114.3 %collective-permute-start.3 = (bf16[384,768]{1,0:T(8,128)(2,1)}, bf16[384,768]{1,0:T(8,128)(2,1)S(1)}, u32[]{:S(2)}, u32[]{:S(2)}) collective-permute-start(bf16[384,768]{1,0:T(8,128)(2,1)} %wa_ref.4), channel_id=1, source_target_pairs={{0,1},{1,0},{2,3},{3,2},{4,5},{5,4},{6,7},{7,6},{8,9},{9,8},{10,11... | collective-permute-start | bytes 1769480 | tf_op jit(solution)/shard_map/ppermute | solution.py:457
  10.3 8.3 %copy-start.14 = (bf16[128,2304]{1,0:T(8,128)(2,1)S(1)}, bf16[128,2304]{1,0:T(8,128)(2,1)}, u32[]{:S(2)}) copy-start(bf16[128,2304]{1,0:T(8,128)(2,1)} %param.21) | copy-start | bytes 1769476
  10.3 9.2 %copy-start.16 = (f32[768]{0:T(1024)S(1)}, f32[768]{0:T(1024)}, u32[]{:S(2)}) copy-start(f32[768]{0:T(1024)} %param.16) | copy-start | bytes 9220
  11.5 58.7 %collective-permute-start.1 = (bf16[512,768]{1,0:T(8,128)(2,1)S(1)}, bf16[512,768]{1,0:T(8,128)(2,1)}, u32[]{:S(2)}, u32[]{:S(2)}) collective-permute-start(bf16[512,768]{1,0:T(8,128)(2,1)S(1)} %dynamic-slice_bitcast_fusion.2), channel_id=1, source_target_pairs={{0,1},{1,0},{2,3},{3,2},{4,5},{5,4},{6,7},{7,6},{8,9},{9,8},{10,11... | collective-permute-start | bytes 2359304 | tf_op jit(solution)/shard_map/ppermute | solution.py:457
  12.6 45.8 %collective-permute-start = (bf16[512,768]{1,0:T(8,128)(2,1)}, bf16[512,768]{1,0:T(8,128)(2,1)}, u32[]{:S(2)}, u32[]{:S(2)}) collective-permute-start(bf16[512,768]{1,0:T(8,128)(2,1)} %dynamic-slice_bitcast_fusion.3), channel_id=1, source_target_pairs={{0,1},{1,0},{2,3},{3,2},{4,5},{5,4},{6,7},{7,6},{8,9},{9,8},{10,11... | collective-permute-start | bytes 2359304 | tf_op jit(solution)/shard_map/ppermute | solution.py:457
  14.5 81.8 %collective-permute-start.2 = (bf16[3,768,384]{2,1,0:T(8,128)(2,1)}, bf16[3,768,384]{2,1,0:T(8,128)(2,1)}, u32[]{:S(2)}, u32[]{:S(2)}) collective-permute-start(bf16[3,768,384]{2,1,0:T(8,128)(2,1)} %wa_ref.5), channel_id=1, source_target_pairs={{0,1},{1,0},{2,3},{3,2},{4,5},{5,4},{6,7},{7,6},{8,9},{9,8},{10,11... | collective-permute-start | bytes 5308424 | tf_op jit(solution)/shard_map/ppermute | solution.py:457
  14.6 139.3 %collective-permute-start.4 = (bf16[768,1536]{1,0:T(8,128)(2,1)}, bf16[768,1536]{1,0:T(8,128)(2,1)}, u32[]{:S(2)}, u32[]{:S(2)}) collective-permute-start(bf16[768,1536]{1,0:T(8,128)(2,1)} %up_ref.1), channel_id=1, source_target_pairs={{0,1},{1,0},{2,3},{3,2},{4,5},{5,4},{6,7},{7,6},{8,9},{9,8},{10,11... | collective-permute-start | bytes 7077896 | tf_op jit(solution)/shard_map/ppermute | solution.py:457
  58.4 138.1 %collective-permute-start.5 = (bf16[1536,768]{1,0:T(8,128)(2,1)}, bf16[1536,768]{1,0:T(8,128)(2,1)S(1)}, u32[]{:S(2)}, u32[]{:S(2)}) collective-permute-start(bf16[1536,768]{1,0:T(8,128)(2,1)} %down_ref.1), channel_id=1, source_target_pairs={{0,1},{1,0},{2,3},{3,2},{4,5},{5,4},{6,7},{7,6},{8,9},{9,8},{10,11... | collective-permute-start | bytes 7077896 | tf_op jit(solution)/shard_map/ppermute | solution.py:457
  63.1 7.1 %copy-start.10 = (bf16[2,512,768]{2,1,0:T(8,128)(2,1)S(1)}, bf16[2,512,768]{2,1,0:T(8,128)(2,1)}, u32[]{:S(2)}) copy-start(bf16[2,512,768]{2,1,0:T(8,128)(2,1)} %param.23) | copy-start | bytes 4718596
  121.6 0.8 copy-start.2
  196.5 1.4 copy-start.17
  220.6 156.4 %collective-permute-start.10 = (bf16[768,1536]{1,0:T(8,128)(2,1)}, bf16[768,1536]{1,0:T(8,128)(2,1)S(1)}, u32[]{:S(2)}, u32[]{:S(2)}) collective-permute-start(bf16[768,1536]{1,0:T(8,128)(2,1)} %get-tuple-element.84), channel_id=1, source_target_pairs={{0,1},{1,0},{2,3},{3,2},{4,5},{5,4},{6,7},{7,6},{8,9},{9,8},{10,11... | collective-permute-start | bytes 7077896 | tf_op jit(solution)/shard_map/ppermute | solution.py:457
  222.3 157.4 %collective-permute-start.11 = (bf16[1536,768]{1,0:T(8,128)(2,1)}, bf16[1536,768]{1,0:T(8,128)(2,1)S(1)}, u32[]{:S(2)}, u32[]{:S(2)}) collective-permute-start(bf16[1536,768]{1,0:T(8,128)(2,1)} %get-tuple-element.86), channel_id=1, source_target_pairs={{0,1},{1,0},{2,3},{3,2},{4,5},{5,4},{6,7},{7,6},{8,9},{9,8},{10,11... | collective-permute-start | bytes 7077896 | tf_op jit(solution)/shard_map/ppermute | solution.py:457
  275.6 19.1 %copy-start.18 = (bf16[384,768]{1,0:T(8,128)(2,1)S(1)}, bf16[384,768]{1,0:T(8,128)(2,1)}, u32[]{:S(2)}) copy-start(bf16[384,768]{1,0:T(8,128)(2,1)} %get-tuple-element.82) | copy-start | bytes 1769476
  275.6 98.7 %copy-start.13 = (bf16[384,768]{1,0:T(8,128)(2,1)S(1)}, bf16[384,768]{1,0:T(8,128)(2,1)}, u32[]{:S(2)}) copy-start(bf16[384,768]{1,0:T(8,128)(2,1)} %get-tuple-element.81) | copy-start | bytes 1769476
  293.0 82.4 %copy-start.8 = (bf16[3,768,384]{2,1,0:T(8,128)(2,1)S(1)}, bf16[3,768,384]{2,1,0:T(8,128)(2,1)}, u32[]{:S(2)}) copy-start(bf16[3,768,384]{2,1,0:T(8,128)(2,1)} %get-tuple-element.79) | copy-start | bytes 5308420
  293.0 82.3 %collective-permute-start.8 = (bf16[3,768,384]{2,1,0:T(8,128)(2,1)}, bf16[3,768,384]{2,1,0:T(8,128)(2,1)S(1)}, u32[]{:S(2)}, u32[]{:S(2)}) collective-permute-start(bf16[3,768,384]{2,1,0:T(8,128)(2,1)} %get-tuple-element.80), channel_id=1, source_target_pairs={{0,1},{1,0},{2,3},{3,2},{4,5},{5,4},{6,7},{7,6},{8,9},{9,8},{10,11... | collective-permute-start | bytes 5308424 | tf_op jit(solution)/shard_map/ppermute | solution.py:457
  294.7 79.6 %collective-permute-start.9 = (bf16[384,768]{1,0:T(8,128)(2,1)S(1)}, bf16[384,768]{1,0:T(8,128)(2,1)S(1)}, u32[]{:S(2)}, u32[]{:S(2)}) collective-permute-start(bf16[384,768]{1,0:T(8,128)(2,1)S(1)} %copy-done.18), channel_id=1, source_target_pairs={{0,1},{1,0},{2,3},{3,2},{4,5},{5,4},{6,7},{7,6},{8,9},{9,8},{10,11... | collective-permute-start | bytes 1769480 | tf_op jit(solution)/shard_map/ppermute | solution.py:457
  375.3 2.3 copy-start.4
  377.6 2.1 copy-start.3
  381.8 0.7 copy-start.15
  381.8 1.7 copy-start.11
  381.8 83.9 %copy-start.12 = (bf16[1024,768]{1,0:T(8,128)(2,1)S(1)}, bf16[1024,768]{1,0:T(8,128)(2,1)}, u32[]{:S(2)}) copy-start(bf16[1024,768]{1,0:T(8,128)(2,1)} %get-tuple-element.76) | copy-start | bytes 4718596
  383.6 86.6 %collective-permute-start.6 = (bf16[512,768]{1,0:T(8,128)(2,1)S(1)}, bf16[512,768]{1,0:T(8,128)(2,1)S(1)}, u32[]{:S(2)}, u32[]{:S(2)}) collective-permute-start(bf16[512,768]{1,0:T(8,128)(2,1)S(1)} %dynamic-slice_bitcast_fusion.1), channel_id=1, source_target_pairs={{0,1},{1,0},{2,3},{3,2},{4,5},{5,4},{6,7},{7,6},{8,9},{9,8},{10,11... | collective-permute-start | bytes 2359304 | tf_op jit(solution)/shard_map/ppermute | solution.py:457
  465.7 16.7 %collective-permute-start.7 = (bf16[512,768]{1,0:T(8,128)(2,1)S(1)}, bf16[512,768]{1,0:T(8,128)(2,1)S(1)}, u32[]{:S(2)}, u32[]{:S(2)}) collective-permute-start(bf16[512,768]{1,0:T(8,128)(2,1)S(1)} %dynamic-slice_bitcast_fusion), channel_id=1, source_target_pairs={{0,1},{1,0},{2,3},{3,2},{4,5},{5,4},{6,7},{7,6},{8,9},{9,8},{10,11... | collective-permute-start | bytes 2359304 | tf_op jit(solution)/shard_map/ppermute | solution.py:457
  536.2 2.3 copy-start.7
  538.5 2.8 copy-start.6
  541.3 2.8 copy-start.5
  544.1 2.5 copy-start.1
Sparse Core Ops, SparseCore 0:
  381.9 154.2 all-reduce.2

commit v2 on v1

v2 whole, which is shorter than its diff:
```python
import functools
import math

import jax
import jax.numpy as jnp
import numpy as np
from jax import lax
from jax.experimental import pallas as pl
from jax.experimental.pallas import tpu as pltpu
from jax.sharding import PartitionSpec as P

HD = 64
TEMB = 128
EPS = 1e-05
MASKED = -1000000000.0
f32 = jnp.float32
bf16 = jnp.bfloat16
VMEM_LIMIT = 56 * 1024 * 1024


def dot_nn(a, b):
    return lax.dot_general(a, b, (((1,), (0,)), ((), ())), preferred_element_type=f32)


def dot_nt(a, b):
    return lax.dot_general(a, b, (((1,), (1,)), ((), ())), preferred_element_type=f32)


def dot_tn(a, b):
    return lax.dot_general(a, b, (((0,), (0,)), ((), ())), preferred_element_type=f32)


def norm_parts(values):
    centred = values - jnp.mean(values, axis=-1, keepdims=True)
    variance = jnp.mean(centred * centred, axis=-1, keepdims=True)
    inverse = lax.rsqrt(variance + EPS)
    return centred * inverse, inverse


def norm_back(grad, normed, inverse):
    return inverse * (
        grad
        - jnp.mean(grad, axis=-1, keepdims=True)
        - normed * jnp.mean(grad * normed, axis=-1, keepdims=True)
    )


def rotary_np(length):
    half = HD // 2
    position = np.arange(length, dtype=np.float32)
    frequency = (10000.0 ** (-np.arange(half, dtype=np.float32) / half)).astype(np.float32)
    angles = position[:, None] * frequency[None, :]
    cosine, sine = np.cos(angles), np.sin(angles)
    cosine = np.concatenate([cosine, cosine] * 2, axis=1).astype(np.float32)
    sine = np.concatenate([-sine, sine] * 2, axis=1).astype(np.float32)
    return cosine, sine


def swap_halves(values):
    lane = lax.broadcasted_iota(jnp.int32, values.shape, 1)
    first = (lane % HD) < (HD // 2)
    return jnp.where(first, pltpu.roll(values, 128 - HD // 2, 1), pltpu.roll(values, HD // 2, 1))


def params(**kw):
    return pltpu.CompilerParams(vmem_limit_bytes=VMEM_LIMIT, **kw)


def cost(flops, nbytes, trans=0):
    return pl.CostEstimate(flops=int(flops), bytes_accessed=int(nbytes), transcendentals=int(trans))


BITS = (1, 2, 4, 8)
MESH = pl.DeviceIdType.MESH


class Place:
    def __init__(self):
        self.me = lax.axis_index("dp")
        self.side = lax.axis_index("tensor")
        self.bits = [(self.me // bit) % 2 for bit in BITS]
        self.partners = [{"dp": self.me + bit * (1 - 2 * b)} for bit, b in zip(BITS, self.bits)]
        self.across = {"tensor": 1 - self.side}

    def greet(self, partners):
        barrier = pltpu.get_barrier_semaphore()
        for partner in partners:
            pl.semaphore_signal(barrier, inc=1, device_id=partner, device_id_type=MESH)
        pl.semaphore_wait(barrier, len(partners))


def remote(src, dst, send, recv, partner):
    return pltpu.make_async_remote_copy(
        src_ref=src, dst_ref=dst, send_sem=send, recv_sem=recv, device_id=partner, device_id_type=MESH
    )


class Reducer:
    STAGES = 5

    def __init__(self, place, chunks, received, sends, recvs):
        self.place, self.chunks, self.received = place, chunks, received
        self.sends, self.recvs = sends, recvs
        self.rows = chunks.shape[2]

    @staticmethod
    def scratch(count, rows, cols):
        shapes = [
            (count, 2, rows // 2, cols),
            (count, 2, rows // 4, cols),
            (count, rows // 4, cols),
            (count, rows // 8, cols),
            (count, rows // 16, cols),
        ]
        return (
            [pltpu.VMEM((count, 2, rows, cols), bf16)]
            + [pltpu.VMEM(shape, bf16) for shape in shapes]
            + [pltpu.SemaphoreType.DMA((count, 5)), pltpu.SemaphoreType.DMA((count, 5))]
        )

    def spans(self, stage):
        core, y, zl, zh = self.place.bits
        r = self.rows
        base = 0
        bits = {0: core, 1: y, 3: zl, 4: zh}
        sizes = {0: r // 2, 1: r // 4, 3: r // 8, 4: r // 16}
        for s in (0, 1, 3, 4):
            if s < stage:
                base = base + bits[s] * sizes[s]
        if stage == 2:
            span = pl.ds(pl.multiple_of(base, 16), r // 4)
            return span, span, self.place.across
        n = sizes[stage]
        keep = pl.ds(pl.multiple_of(base + bits[stage] * n, 16), n)
        send = pl.ds(pl.multiple_of(base + (1 - bits[stage]) * n, 16), n)
        return keep, send, self.place.partners[{0: 0, 1: 1, 3: 2, 4: 3}[stage]]

    def copy(self, stage, c):
        _, send, partner = self.spans(stage)
        if stage < 2:
            source = self.chunks.at[c, :, send, :]
        else:
            source = self.chunks.at[c, 1 if stage == 2 else 0, send, :]
        return remote(
            source, self.received[stage].at[c], self.sends.at[c, stage], self.recvs.at[c, stage], partner
        )

    def start(self, stage, c):
        self.copy(stage, c).start()

    def finish(self, stage, c, put=None):
        self.copy(stage, c).wait()
        keep, _, _ = self.spans(stage)
        came = self.received[stage]
        if stage < 2:
            for half in range(2):
                self.chunks[c, half, keep, :] += came[c, half]
        elif stage < 4:
            self.chunks[c, 0, keep, :] += came[c]
        else:
            put(c, self.chunks[c, 0, keep, :] + came[c])


class Gatherer:
    STAGES = 4

    def __init__(self, place, array, dim, sends, recvs):
        self.place, self.array, self.dim, self.sends, self.recvs = place, array, dim, sends, recvs
        core, y, zl, zh = place.bits
        n = array.shape[dim] // 16
        self.size = n
        self.bases = [
            core * 8 + y * 4 + zl * 2 + zh,
            core * 8 + y * 4 + zl * 2,
            core * 8 + y * 4,
            core * 8,
        ]

    def view(self, stage):
        n = self.size
        span = pl.ds(pl.multiple_of(self.bases[stage] * n, 16), 2**stage * n)
        return self.array.at[(slice(None),) * self.dim + (span,)]

    def copy(self, stage):
        span = self.view(stage)
        return remote(
            span, span, self.sends.at[stage], self.recvs.at[stage], self.place.partners[3 - stage]
        )

    def start(self, stage):
        self.copy(stage).start()

    def finish(self, stage):
        self.copy(stage).wait()


def qkv_rows(row, rows, x_ref, gain_ref, w_ref, cos_ref, sin_ref, n_ref, q_ref, k_ref, v_ref, first):
    span = pl.ds(row, rows)
    pairs = w_ref.shape[2] // 128
    if n_ref is None:
        normed = x_ref[span, :]
    else:
        normed, _ = norm_parts(x_ref[span, :].astype(f32))
        normed = (normed * gain_ref[...]).astype(bf16)
        n_ref[span, :] = normed
    cosine, sine = cos_ref[span, :], sin_ref[span, :]
    for which, out in ((0, q_ref), (1, k_ref)):
        raw = dot_nn(normed, w_ref[which])
        for pair in range(pairs):
            part = raw[:, pair * 128 : pair * 128 + 128]
            turned = (part * cosine + swap_halves(part) * sine).astype(bf16)
            if which == 0:
                turned = turned * jnp.asarray(0.125, bf16)
            out[first + pair, span, :] = turned
    raw = dot_nn(normed, w_ref[2]).astype(bf16)
    for pair in range(pairs):
        v_ref[first + pair, span, :] = raw[:, pair * 128 : pair * 128 + 128]


def attend_rows(pair, row, rows, q_ref, k_ref, v_ref, segc_ref, segr_ref, o_ref, lse_ref):
    lane = lax.broadcasted_iota(jnp.int32, (1, 128), 1)
    low = lane < HD
    span = pl.ds(row, rows)
    q, k, v = q_ref[pair, span, :], k_ref[pair], v_ref[pair]
    mask = segc_ref[span, :] == segr_ref[...]
    parts = []
    for head in range(2):
        mine = low if head == 0 else jnp.logical_not(low)
        scores = dot_nt(jnp.where(mine, q, jnp.zeros_like(q)), k)
        scores = jnp.where(mask, scores, MASKED)
        largest = jnp.max(scores, axis=1, keepdims=True)
        weights = jnp.exp(scores - largest).astype(bf16)
        mixed = dot_nn(weights, jnp.where(mine, v, jnp.ones_like(v)))
        total = pltpu.roll(mixed, HD, 1)
        parts.append((mixed / total, largest + jnp.log(total)))
    o_ref[span, pl.ds(pl.multiple_of(pair * 128, 128), 128)] = jnp.where(
        low, parts[0][0], parts[1][0]
    ).astype(bf16)
    lse = jnp.where(low, parts[0][1], parts[1][1]).T
    lse_ref[pair, 0:1, span] = lse[0:1, :]
    lse_ref[pair, 1:2, span] = lse[HD : HD + 1, :]


def front_kernel(
    tok, cot, wq, wo, wu, wd, gain_ref, segc_ref, segr_ref, cos_ref, sin_ref,
    x_out, cot_out, n_out, q_out, k_out, v_out, o_out, lse_out, oq, oo, ou, od,
    xs, ns, qs, ks, vs, os, ls, wbuf, local, xsend, xrecv, wsend, wrecv,
):
    place = Place()
    core, y = place.bits[0], place.bits[1]
    side = place.side
    length, half = xs.shape[0], xs.shape[0] // 2
    rows = 256
    place.greet([place.across, place.partners[0], place.partners[1]])

    own_rows = pl.ds(pl.multiple_of(side * half, half), half)
    send_tok = remote(tok.at[1 - side], xs.at[own_rows, :], xsend.at[0], xrecv.at[0], place.across)
    send_tok.start()
    send_cot = remote(cot.at[1 - side], cot_out.at[own_rows, :], xsend.at[1], xrecv.at[1], place.across)

    groups = ((wq, oq), (wo, oo), (wu, ou), (wd, od))

    def quarter(ref, index):
        if len(ref.shape) == 3:
            n = ref.shape[1] // 4
            return ref.at[:, pl.ds(pl.multiple_of(index * n, 16), n), :]
        n = ref.shape[0] // 4
        return ref.at[pl.ds(pl.multiple_of(index * n, 16), n), :]

    mine = core + 2 * y
    facing = core + 2 * (1 - y)

    def fetch(group, stage):
        own, other = groups[group]
        if stage == 0:
            src, dst, partner = quarter(own, mine), quarter(other, mine), place.across
        elif stage == 1:
            src, dst, partner = quarter(other, mine), quarter(other, mine), place.partners[1]
        elif stage == 2:
            src, dst, partner = quarter(other, mine), quarter(other, mine), place.partners[0]
        else:
            src, dst, partner = quarter(other, facing), quarter(other, facing), place.partners[0]
        return remote(src, dst, wsend.at[group, stage], wrecv.at[group, stage], partner)

    locals_ = []

    def copy_here(src, dst, index):
        c = pltpu.make_async_copy(src, dst, local.at[index])
        c.start()
        return c

    get_x = copy_here(tok.at[side], xs.at[own_rows, :], 0)
    get_w = copy_here(wq, wbuf, 1)
    put_cot = copy_here(cot.at[side], cot_out.at[own_rows, :], 2)
    fetch(0, 0).start()
    get_x.wait()
    get_w.wait()

    def qkv_half(base, w_first, n_ref):
        def step(i, carry):
            row = pl.multiple_of(base + i * rows, rows)
            qkv_rows(
                row, rows, xs if n_ref is not None else ns, gain_ref, wbuf, cos_ref, sin_ref,
                n_ref, qs, ks, vs, w_first,
            )
            return carry

        lax.fori_loop(0, half // rows, step, 0)

    qkv_half(side * half, 0, ns)
    send_tok.wait()
    fetch(1, 0).start()
    fetch(2, 0).start()
    qkv_half((1 - side) * half, 0, ns)
    put_x = copy_here(xs, x_out, 3)
    put_n = copy_here(ns, n_out, 4)
    fetch(0, 0).wait()
    fetch(0, 1).start()
    fetch(0, 2).start()

    def attend(pair, carry):
        @pl.when(pair == 1)
        def _():
            fetch(0, 1).wait()
            fetch(0, 3).start()
            fetch(1, 0).wait()
            fetch(1, 1).start()
            fetch(1, 2).start()

        @pl.when(pair == 2)
        def _():
            fetch(2, 0).wait()
            fetch(2, 1).start()
            fetch(2, 2).start()
            fetch(3, 0).start()

        @pl.when(pair == 3)
        def _():
            fetch(0, 2).wait()
            fetch(0, 3).wait()
            copy = pltpu.make_async_copy(oq, wbuf, local.at[1])
            copy.start()
            copy.wait()
            qkv_half(0, 3, None)
            qkv_half(half, 3, None)

        @pl.when(pair == 4)
        def _():
            send_cot.start()
            fetch(1, 1).wait()
            fetch(1, 3).start()
            fetch(2, 1).wait()
            fetch(2, 3).start()
            fetch(3, 0).wait()
            fetch(3, 1).start()
            fetch(3, 2).start()

        for block in range(length // rows):
            attend_rows(pair, block * rows, rows, qs, ks, vs, segc_ref, segr_ref, os, ls)
        return carry

    lax.fori_loop(0, 6, attend, 0)
    fetch(3, 1).wait()
    fetch(3, 3).start()
    ends = [
        copy_here(qs, q_out, 5),
        copy_here(ks, k_out, 6),
        copy_here(vs, v_out, 7),
        copy_here(os, o_out, 8),
        copy_here(ls, lse_out, 9),
    ]
    for c in [put_cot, put_x, put_n] + ends:
        c.wait()
    fetch(1, 2).wait()
    fetch(1, 3).wait()
    fetch(2, 2).wait()
    fetch(2, 3).wait()
    fetch(3, 2).wait()
    fetch(3, 3).wait()
    send_cot.wait()


def front_call(tokens, cot, wq, wo, wu, wd, gain, segc, segr, cosine, sine):
    length, width = 2 * tokens.shape[1], tokens.shape[2]
    any_ = pl.BlockSpec(memory_space=pl.ANY)
    vm = pl.BlockSpec(memory_space=pltpu.VMEM)
    shape = jax.ShapeDtypeStruct
    pairs = width // 128
    return pl.pallas_call(
        front_kernel,
        in_specs=[any_] * 6 + [vm] * 5,
        out_specs=[any_] * 12,
        out_shape=[
            shape((length, width), bf16),
            shape((length, width), bf16),
            shape((length, width), bf16),
            shape((pairs, length, 128), bf16),
            shape((pairs, length, 128), bf16),
            shape((pairs, length, 128), bf16),
            shape((length, width), bf16),
            shape((pairs, 8, length), f32),
            shape(wq.shape, bf16),
            shape(wo.shape, bf16),
            shape(wu.shape, bf16),
            shape(wd.shape, bf16),
        ],
        scratch_shapes=[
            pltpu.VMEM((length, width), bf16),
            pltpu.VMEM((length, width), bf16),
            pltpu.VMEM((pairs, length, 128), bf16),
            pltpu.VMEM((pairs, length, 128), bf16),
            pltpu.VMEM((pairs, length, 128), bf16),
            pltpu.VMEM((length, width), bf16),
            pltpu.VMEM((pairs, 8, length), f32),
            pltpu.VMEM(wq.shape, bf16),
            pltpu.SemaphoreType.DMA((10,)),
            pltpu.SemaphoreType.DMA((2,)),
            pltpu.SemaphoreType.DMA((2,)),
            pltpu.SemaphoreType.DMA((4, 4)),
            pltpu.SemaphoreType.DMA((4, 4)),
        ],
        compiler_params=params(collective_id=0, has_side_effects=True),
        name="front",
    )(tokens, cot, wq, wo, wu, wd, gain, segc, segr, cosine, sine)


def gelu_both(u):
    c0 = math.sqrt(2.0 / math.pi)
    square = u * u
    t = jnp.tanh(u * (c0 + (c0 * 0.044715) * square))
    half = 0.5 + 0.5 * t
    act = u * half
    slope = half + (0.5 * u) * (1.0 - t * t) * (c0 + (3.0 * c0 * 0.044715) * square)
    return act, slope


FEED_STEPS = 6


def feed_kernel(
    x_ref, cot_ref, o_ref, woa_ref, wob_ref, mod_ref, upa_ref, upb_ref, downa_ref, downb_ref,
    mixed_ref, dhidden_ref, do_ref, dwo_ref, sums_ref, finup_ref, findown_ref,
    hidden, modul, dbranch, modul_t, branch, dmod, acts, dups, *reducing,
):
    step = pl.program_id(0)
    place = Place()
    length, width = x_ref.shape
    block = upa_ref.shape[1]
    rows = 256
    blocks = length // rows
    half = woa_ref.shape[0]
    ups, downs = reducing[0], reducing[8]
    reducers = [Reducer(place, a[0], a[1:6], a[6], a[7]) for a in (reducing[:8], reducing[8:])]

    def put_up(c, value):
        finup_ref[:, pl.ds(pl.multiple_of(c * block, 128), block)] = value

    def put_down(c, value):
        findown_ref[c] = value

    puts = (put_up, put_down)

    @pl.when(step == 0)
    def _():
        place.greet(place.partners + [place.across])
        shift, scale, gate = mod_ref[0:1, :], mod_ref[1:2, :], mod_ref[2:3, :]

        def rows_of(i, carry):
            span = pl.ds(pl.multiple_of(i * rows, rows), rows)
            h = x_ref[span, :].astype(f32) + (
                dot_nn(o_ref[span, :half], woa_ref[...]) + dot_nn(o_ref[span, half:], wob_ref[...])
            )
            hidden[span, :] = h
            normed, _ = norm_parts(h)
            m = (normed * (1.0 + scale) + shift).astype(bf16)
            modul[span, :] = m
            modul_t[:, span] = m.T
            d = (cot_ref[span, :].astype(f32) * gate).astype(bf16)
            dbranch[span, :] = d
            branch[span, :] = jnp.zeros((rows, width), f32)
            dmod[span, :] = jnp.zeros((rows, width), f32)
            return carry

        lax.fori_loop(0, blocks, rows_of, 0)

    for stage in range(Reducer.STAGES):
        c = step - 1 - stage

        @pl.when(jnp.logical_and(c >= 0, c < FEED_STEPS))
        def _(stage=stage, c=c):
            for reducer, put in zip(reducers, puts):
                reducer.finish(stage, c, put)
                if stage + 1 < Reducer.STAGES:
                    reducer.start(stage + 1, c)

    @pl.when(step < FEED_STEPS)
    def _():
        up = jnp.concatenate([upa_ref[...], upb_ref[...]], axis=1)
        down = jnp.concatenate([downa_ref[...], downb_ref[...]], axis=0)
        for i in range(blocks):
            span = pl.ds(i * rows, rows)
            u = dot_nn(modul[span, :], up)
            act, slope = gelu_both(u)
            act = act.astype(bf16)
            acts[span, :] = act
            d_act = dot_nt(dbranch[span, :], down)
            d_up = (d_act * slope).astype(bf16)
            dups[span, :] = d_up
            branch[span, :] += dot_nn(act, down)
            dmod[span, :] += dot_nt(d_up, up)
        grad = dot_nn(modul_t[...], dups[...]).astype(bf16)
        ups[step, 0] = grad[:, :block]
        ups[step, 1] = grad[:, block:]
        reducers[0].start(0, step)
        grad = dot_tn(acts[...], dbranch[...]).astype(bf16)
        downs[step, 0] = grad[:block]
        downs[step, 1] = grad[block:]
        reducers[1].start(0, step)

    @pl.when(step == FEED_STEPS)
    def _():
        sums_ref[...] = jnp.zeros_like(sums_ref)

    @pl.when(jnp.logical_and(step >= FEED_STEPS, step < FEED_STEPS + blocks))
    def _():
        span = pl.ds(pl.multiple_of((step - FEED_STEPS) * rows, rows), rows)
        scale, gate = mod_ref[1:2, :], mod_ref[2:3, :]
        h = hidden[span, :]
        dout = cot_ref[span, :].astype(f32)
        br = branch[span, :]
        mixed_ref[span, :] = (h + gate * br).astype(bf16)
        normed, inverse = norm_parts(h)
        dm = dmod[span, :]
        sums_ref[0:1, :] += jnp.sum(dm, axis=0, keepdims=True)
        sums_ref[1:2, :] += jnp.sum(dm * normed, axis=0, keepdims=True)
        sums_ref[2:3, :] += jnp.sum(dout * br, axis=0, keepdims=True)
        dh = dout + norm_back(dm * (1.0 + scale), normed, inverse)
        dhidden_ref[span, :] = dh
        dattn = dh.astype(bf16)
        modul[span, :] = dattn
        do_ref[span, :half] = dot_nt(dattn, woa_ref[...]).astype(bf16)
        do_ref[span, half:] = dot_nt(dattn, wob_ref[...]).astype(bf16)

    @pl.when(step == FEED_STEPS + blocks)
    def _():
        for i in range(2):
            grad = dot_tn(o_ref[:, i * half : (i + 1) * half], modul[...]).astype(bf16)
            dwo_ref[i, :half, :] = grad[:, :half]
            dwo_ref[i, half:, :] = grad[:, half:]


def feed_call(x, cot, o, woa, wob, mod, upa, upb, downa, downb):
    length, width = x.shape
    hidden = upa.shape[1]
    block = hidden // FEED_STEPS
    half = woa.shape[0]
    last = FEED_STEPS - 1

    def const(shape):
        zeros = (0,) * len(shape)
        return pl.BlockSpec(shape, lambda j: zeros, pipeline_mode=pl.Buffered(1))

    ups = pl.BlockSpec((width, block), lambda j: (0, jnp.minimum(j, last)))
    downs = pl.BlockSpec((block, width), lambda j: (jnp.minimum(j, last), 0))
    shape = jax.ShapeDtypeStruct
    outs = [
        shape((length, width), bf16),
        shape((length, width), f32),
        shape((length, width), bf16),
        shape((2, width, half), bf16),
        shape((8, width), f32),
        shape((width // 16, hidden), bf16),
        shape((FEED_STEPS, block // 16, width), bf16),
    ]
    return pl.pallas_call(
        feed_kernel,
        grid=(FEED_STEPS + length // 256 + 1,),
        in_specs=[const(a.shape) for a in (x, cot, o, woa, wob, mod)] + [ups, ups, downs, downs],
        out_specs=[const(o.shape) for o in outs],
        out_shape=outs,
        scratch_shapes=[
            pltpu.VMEM((length, width), f32),
            pltpu.VMEM((length, width), bf16),
            pltpu.VMEM((length, width), bf16),
            pltpu.VMEM((width, length), bf16),
            pltpu.VMEM((length, width), f32),
            pltpu.VMEM((length, width), f32),
            pltpu.VMEM((length, 2 * block), bf16),
            pltpu.VMEM((length, 2 * block), bf16),
        ]
        + Reducer.scratch(FEED_STEPS, width, block)
        + Reducer.scratch(FEED_STEPS, block, width),
        compiler_params=params(collective_id=1, has_side_effects=True),
        name="feed",
    )(x, cot, o, woa, wob, mod, upa, upb, downa, downb)


def attend_back(
    q_ref, k_ref, v_ref, o_ref, do_ref, lse_ref, segc_ref, segr_ref, cos_ref, sin_ref, acc_ref, put
):
    length = o_ref.shape[0]
    rows = 256
    lane = lax.broadcasted_iota(jnp.int32, (1, 128), 1)
    low = lane < HD
    q, do = q_ref[0], do_ref[...]
    product = do.astype(f32) * o_ref[...].astype(f32)
    high_part = product.astype(bf16)
    low_part = (product - high_part.astype(f32)).astype(bf16)
    row8 = lax.broadcasted_iota(jnp.int32, (8, 128), 0)
    lane8 = lax.broadcasted_iota(jnp.int32, (8, 128), 1)
    select = jnp.where((lane8 // HD) == row8, 1.0, 0.0).astype(bf16)
    delta = dot_nt(select, high_part) + dot_nt(select, low_part)
    lse = lse_ref[0]
    segr = segr_ref[...]
    zero = jnp.zeros_like(q)
    q_heads = (jnp.where(low, q, zero), jnp.where(low, zero, q))
    do_heads = (jnp.where(low, do, zero), jnp.where(low, zero, do))
    acc_ref[...] = jnp.zeros_like(acc_ref)
    for block in range(length // rows):
        span = pl.ds(block * rows, rows)
        k, v = k_ref[0, span, :], v_ref[0, span, :]
        mask = segc_ref[span, :] == segr
        dv = jnp.zeros((rows, 128), f32)
        dk = jnp.zeros((rows, 128), f32)
        dq = jnp.zeros((128, length), f32)
        for head in range(2):
            mine = low if head == 0 else jnp.logical_not(low)
            kh = jnp.where(mine, k, jnp.zeros_like(k))
            vh = jnp.where(mine, v, jnp.zeros_like(v))
            scores = jnp.where(mask, dot_nt(kh, q), MASKED)
            probs = jnp.exp(scores - lse[head : head + 1, :])
            dv = dv + dot_nn(probs.astype(bf16), do_heads[head])
            d_probs = dot_nt(vh, do)
            d_scores = (probs * (d_probs - delta[head : head + 1, :])).astype(bf16)
            dk = dk + dot_nn(d_scores, q_heads[head])
            dq = dq + dot_tn(kh, d_scores)
        acc_ref[...] += dq
        cosine, sine = cos_ref[span, :], sin_ref[span, :]
        put(1, span, (dk * cosine - swap_halves(dk) * sine).astype(bf16))
        put(2, span, dv.astype(bf16))
    dq = acc_ref[...].T * 0.125
    put(0, slice(None), (dq * cos_ref[...] - swap_halves(dq) * sin_ref[...]).astype(bf16))


def back_kernel(
    q_ref, k_ref, v_ref, o_ref, do_ref, lse_ref, segc_ref, segr_ref, cos_ref, sin_ref,
    n_ref, x_ref, gain_ref, dhidden_ref, wa_ref, wb_ref, dwo_ref, small_ref, mixed_in, up_in, down_in,
    up_out, down_out, out_out, qkv_out, mixed_out, dtok_out, every_out, dgain_ref,
    n_t, draw, acc, dtok, fin_out, fin_qkv, every_ref, gains, gains_in,
    chunks, r0, r1, r2, r3, r4, sends, recvs,
    fsend, frecv, asend, arecv, gsend, grecv, ssend, srecv, xsend, xrecv, local,
):
    step = pl.program_id(0)
    place = Place()
    side = place.side
    length, width = x_ref.shape
    half_len = length // 2
    rows = 256
    blocks = length // rows
    half = wa_ref.shape[2]
    reducer = Reducer(place, chunks, (r0, r1, r2, r3, r4), sends, recvs)
    gather_ffn = [
        Gatherer(place, up_out, 0, fsend.at[0], frecv.at[0]),
        Gatherer(place, down_out, 1, fsend.at[1], frecv.at[1]),
    ]
    gather_att = [
        Gatherer(place, out_out, 0, asend.at[0], arecv.at[0]),
        Gatherer(place, qkv_out, 1, asend.at[1], arecv.at[1]),
    ]
    own_rows = pl.ds(pl.multiple_of(side * half_len, half_len), half_len)
    other_rows = pl.ds(pl.multiple_of((1 - side) * half_len, half_len), half_len)
    order = [place.across] + place.partners

    send_mixed = remote(mixed_in.at[other_rows, :], mixed_out.at[side], xsend.at[0], xrecv.at[0], place.across)
    keep_mixed = pltpu.make_async_copy(mixed_in.at[own_rows, :], mixed_out.at[side], local.at[0])
    send_dtok = remote(dtok.at[other_rows, :], dtok_out.at[side], xsend.at[1], xrecv.at[1], place.across)
    keep_dtok = pltpu.make_async_copy(dtok.at[own_rows, :], dtok_out.at[side], local.at[1])
    put_ffn = [
        pltpu.make_async_copy(up_in, gather_ffn[0].view(0), local.at[2]),
        pltpu.make_async_copy(down_in, gather_ffn[1].view(0), local.at[3]),
    ]
    put_att = [
        pltpu.make_async_copy(fin_out, gather_att[0].view(0), local.at[4]),
        pltpu.make_async_copy(fin_qkv, gather_att[1].view(0), local.at[5]),
    ]
    put_every = pltpu.make_async_copy(every_ref, every_out, local.at[6])

    def put_final(c, value):
        if c == 0:
            fin_out[...] = value
        else:
            for which in range(3):
                fin_qkv[which, :, (c - 1) * 128 : c * 128] = value[:, which * 128 : which * 128 + 128]

    number = 2 * place.me % 32 + side

    def spread(stage):
        span = every_ref.at[pl.ds(number - number % 2**stage, 2**stage)]
        return remote(span, span, ssend.at[stage], srecv.at[stage], order[stage])

    def gain_copy(stage):
        return remote(gains.at[stage], gains_in.at[stage], gsend.at[stage], grecv.at[stage], order[stage])

    @pl.when(step == 0)
    def _():
        place.greet(place.partners + [place.across])
        for copy in put_ffn:
            copy.start()
        send_mixed.start()
        keep_mixed.start()
        every_ref[pl.ds(number, 1)] = small_ref[...]
        spread(0).start()
        chunks[0] = dwo_ref[...]
        reducer.start(0, 0)
        for copy, gather in zip(put_ffn, gather_ffn):
            copy.wait()
            gather.start(0)
        n_t[...] = n_ref[...].T

    starts = (0, 1, 3, 5)
    for c in range(4):
        for stage in range(Reducer.STAGES):

            @pl.when(step == starts[c] + 1 + stage)
            def _(c=c, stage=stage):
                reducer.finish(stage, c, put_final)
                if stage + 1 < Reducer.STAGES:
                    reducer.start(stage + 1, c)

    for stage, at in enumerate((1, 3, 5, 7)):

        @pl.when(step == at)
        def _(stage=stage):
            for gather in gather_ffn:
                gather.finish(stage)
                if stage + 1 < Gatherer.STAGES:
                    gather.start(stage + 1)

    for stage in range(5):

        @pl.when(step == stage + 1)
        def _(stage=stage):
            spread(stage).wait()
            if stage < 4:
                spread(stage + 1).start()
            else:
                put_every.start()

    @pl.when(step < 6)
    def _():
        pair = step // 2 + 3 * (step % 2)
        lanes = pl.ds(pl.multiple_of(pair * 128, 128), 128)

        def put(which, span, value):
            draw[which, span, lanes] = value

        attend_back(
            q_ref, k_ref, v_ref, o_ref, do_ref, lse_ref, segc_ref, segr_ref, cos_ref, sin_ref, acc, put
        )
        for which in range(3):
            grad = dot_nn(n_t[...], draw[which, :, lanes]).astype(bf16)
            chunks[1 + step // 2, step % 2, :, which * 128 : which * 128 + 128] = grad

    for c in range(1, 4):

        @pl.when(step == starts[c])
        def _(c=c):
            reducer.start(0, c)

    @pl.when(step == 6)
    def _():
        dgain_ref[...] = jnp.zeros_like(dgain_ref)

    @pl.when(jnp.logical_and(step >= 6, step < 6 + blocks))
    def _():
        span = pl.ds(pl.multiple_of((step - 6) * rows, rows), rows)
        dnormed = jnp.zeros((rows, width), f32)
        for which in range(3):
            dnormed = dnormed + dot_nt(draw[which, span, :half], wa_ref[which])
            dnormed = dnormed + dot_nt(draw[which, span, half:], wb_ref[which])
        normed, inverse = norm_parts(x_ref[span, :].astype(f32))
        dgain_ref[0:1, :] += jnp.sum(dnormed * normed, axis=0, keepdims=True)
        dtok[span, :] = (
            dhidden_ref[span, :] + norm_back(dnormed * gain_ref[...], normed, inverse)
        ).astype(bf16)

    @pl.when(step == 6 + blocks)
    def _():
        send_dtok.start()
        keep_dtok.start()
        for copy in put_att:
            copy.start()
        gains[0] = dgain_ref[...]
        gain_copy(0).start()
        for copy in put_att:
            copy.wait()
        for stage in range(5):
            if stage < 4:
                for gather in gather_att:
                    gather.start(stage)
            gain_copy(stage).wait()
            total = gains[stage] + gains_in[stage]
            if stage < 4:
                gains[stage + 1] = total
                gain_copy(stage + 1).start()
                for gather in gather_att:
                    gather.finish(stage)
            else:
                dgain_ref[...] = total
        send_mixed.wait()
        keep_mixed.wait()
        send_dtok.wait()
        keep_dtok.wait()
        put_every.wait()


def back_call(
    q, k, v, o, do, lse, segc, segr, cosine, sine, n, x, gain, dhidden, wa, wb, dwo, small, mixed, ups, downs
):
    length, width = x.shape
    pairs = width // 128
    half = wa.shape[2]
    shape = jax.ShapeDtypeStruct

    def const(a):
        zeros = (0,) * len(a.shape)
        return pl.BlockSpec(a.shape, lambda s: zeros, pipeline_mode=pl.Buffered(1))

    def pair_of(s):
        s = jnp.minimum(s, 5)
        return s // 2 + 3 * (s % 2)

    any_ = pl.BlockSpec(memory_space=pl.ANY)
    major = pl.BlockSpec((1, length, 128), lambda s: (pair_of(s), 0, 0))
    minor = pl.BlockSpec((length, 128), lambda s: (0, pair_of(s)))
    every = shape((32,) + small.shape[1:], f32)
    dgain = shape((8, width), f32)
    up_all = shape((width, ups.shape[1]), bf16)
    down_all = shape((downs.shape[0], 16 * downs.shape[1], width), bf16)
    out_all = shape((width, half), bf16)
    qkv_all = shape(wa.shape, bf16)
    tok = shape((2, length // 2, width), bf16)
    dma = pltpu.SemaphoreType.DMA
    return pl.pallas_call(
        back_kernel,
        grid=(6 + length // 256 + 1,),
        in_specs=[major] * 3
        + [minor] * 2
        + [pl.BlockSpec((1, 8, length), lambda s: (pair_of(s), 0, 0))]
        + [const(a) for a in (segc, segr, cosine, sine, n, x, gain, dhidden, wa, wb, dwo, small)]
        + [any_, const(ups), const(downs)],
        out_specs=[any_] * 7 + [const(dgain)],
        out_shape=[up_all, down_all, out_all, qkv_all, tok, tok, every, dgain],
        scratch_shapes=[
            pltpu.VMEM((width, length), bf16),
            pltpu.VMEM((3, length, width), bf16),
            pltpu.VMEM((128, length), f32),
            pltpu.VMEM((length, width), bf16),
            pltpu.VMEM((width // 16, half), bf16),
            pltpu.VMEM((3, width // 16, half), bf16),
            pltpu.VMEM(every.shape, f32),
            pltpu.VMEM((5, 8, width), f32),
            pltpu.VMEM((5, 8, width), f32),
        ]
        + Reducer.scratch(4, width, half)
        + [dma((2, 4))] * 4
        + [dma((5,))] * 4
        + [dma((2,)), dma((2,)), dma((7,))],
        compiler_params=params(collective_id=2, has_side_effects=True),
        name="back",
    )(q, k, v, o, do, lse, segc, segr, cosine, sine, n, x, gain, dhidden, wa, wb, dwo, small, mixed, ups, downs)


def time_embedding(timestep):
    half = TEMB // 2
    frequency = jnp.exp(-math.log(10000.0) * jnp.arange(half, dtype=f32) / half)
    angles = timestep.astype(f32)[:, None] * frequency[None, :]
    return jnp.concatenate([jnp.cos(angles), jnp.sin(angles)], axis=-1)


def per_device(
    groups, tokens, segment_ids, timestep, ln_gain, w_qkv, w_out, w_up, w_down, ada_weight, ada_bias, cotangent
):
    half, width = tokens.shape[1], tokens.shape[2]
    length = 2 * half
    side = lax.axis_index("tensor")
    pick = lambda a, i: lax.dynamic_index_in_dim(a, i, 0, keepdims=False)

    segments = pick(segment_ids, side)
    segc, segr = segments.reshape(length, 1), segments.reshape(1, length)
    gain = ln_gain.reshape(1, width)
    cosine, sine = (jnp.asarray(a) for a in rotary_np(length))

    embedding = time_embedding(timestep)
    mine = pick(embedding, side)
    mod = jnp.sum(mine[:, None] * ada_weight.astype(f32), axis=0) + ada_bias
    mod = mod.reshape(3, width)

    x, cot, n, q, k, v, o, lse, o_qkv, o_out, o_up, o_down = front_call(
        tokens, cotangent, w_qkv, w_out, w_up, w_down, gain, segc, segr, cosine, sine
    )
    mixed, dhidden, do, dwo, sums, ups, downs = feed_call(
        x, cot, o, w_out, o_out, mod, w_up, o_up, w_down, o_down
    )
    small = jnp.concatenate(
        [sums[:3].reshape(3 * width // 128, 128), mine[None, :], jnp.zeros((5, 128), f32)]
    )[None]
    d_up, d_down, d_out, d_qkv, mixed, dtok, every, dgain = back_call(
        q, k, v, o, do, lse, segc, segr, cosine, sine, n, x, gain, dhidden, w_qkv, o_qkv, dwo, small, mixed, ups, downs
    )
    rows = 3 * width // 128
    d_mods = every[:, :rows].reshape(32, 3 * width)
    d_ada_weight = jnp.dot(every[:, rows].T, d_mods, precision=lax.Precision.HIGHEST)
    d_ada_bias = jnp.sum(d_mods, axis=0)
    d_gain = dgain[0]

    d_up, d_qkv = d_up.astype(f32), d_qkv.astype(f32)
    d_down = d_down.reshape(-1, width).astype(f32)
    heads = d_out.shape[1]
    d_out = jnp.concatenate([d_out[:heads], d_out[heads:]], axis=1).astype(f32)

    def rest(a):
        bit = 16
        while bit < groups:
            a = a + lax.ppermute(a, "dp", [(i, i ^ bit) for i in range(groups)])
            bit *= 2
        return a

    return (
        mixed,
        dtok,
        rest(d_gain),
        rest(d_qkv),
        rest(d_out),
        rest(d_up),
        rest(d_down),
        rest(d_ada_weight),
        rest(d_ada_bias),
    )


def solution(mesh):
    in_specs = (
        P("dp", "tensor", None),
        P("dp", None),
        P("dp"),
        P(),
        P(None, None, "tensor"),
        P("tensor", None),
        P(None, "tensor"),
        P("tensor", None),
        P(),
        P(),
        P("dp", "tensor", None),
    )
    out_specs = (
        P("dp", "tensor", None),
        P("dp", "tensor", None),
        P(),
        P(None, None, "tensor"),
        P("tensor", None),
        P(None, "tensor"),
        P("tensor", None),
        P(),
        P(),
    )
    return jax.shard_map(
        functools.partial(per_device, mesh.shape["dp"]), mesh=mesh, in_specs=in_specs, out_specs=out_specs, check_vma=False
    )
```

time: 563 us -> 343 us (0.61); the launches traced: 554 us -> 343 us
  waiting for transfers between devices: 226 us -> 0 us
  Pallas kernels: 173 us -> 314 us
  blocking collectives: 80.5 us -> 0 us
  starting transfers between devices: 15.8 us -> 0 us
  other arithmetic: 29.1 us -> 13.8 us
  between operations: 14.7 us -> 0.72 us
    ppermute x12 -> x0, waiting for transfers between devices: 174 us -> none  [swap(): return lax.ppermute(a, 'tensor', SWAP)]
    pallas_call x11 -> x3, Pallas kernels: 173 us -> 314 us  [the longest x1 146 us: back_call(): pl.pallas_call(back_kernel, grid=(6 + length // 256 + 1,), in_specs=[majo...]
    all_gather x1 -> x0, blocking collectives: 80.5 us -> none  [per_device(): every = lax.all_gather(small, ('dp', 'tensor'), axis=0)]
    psum x1 -> x0, waiting for transfers between devices: 52.4 us -> none  [total(): return lax.psum(own + swap(other), 'dp').astype(f32)]
    ppermute x12 -> x0, starting transfers between devices: 15.8 us -> none  [swap(): return lax.ppermute(a, 'tensor', SWAP)]
    add x4 -> x0, other arithmetic: 6.71 us -> none  [total(): return lax.psum(own + swap(other), 'dp').astype(f32)]
  transfers between devices with their start and end apart: 13 -> 0, of which waited for: 6 -> 0; matrix products, arithmetic and copies ran while one was open for 5% -> 0% of each run, Pallas kernels for 27% -> 0%
where the time goes in v2:
time: 343 us
  Pallas kernels  314 us (92%)
  other arithmetic  13.8 us (4%)
  local copies, waits for them, and re-layouts  11.7 us (3%)
    pallas_call x1, Pallas kernels, back_call(): pl.pallas_call(back_kernel, grid=(6 + length // 256 + 1,), in_specs=[majo...  146 us
    pallas_call x1, Pallas kernels, feed_call(): pl.pallas_call(feed_kernel, grid=(FEED_STEPS + length // 256 + 1,), in_sp...  88.3 us
    pallas_call x1, Pallas kernels, front_call(): pl.pallas_call(front_kernel, in_specs=[any_] * 6 + [vm] * 5, out_specs=[a...  80.3 us

profile of v2, /device:TPU:0, one launch (start us, length us, event | category | flops | bytes accessed | tf_op | source)
XLA Modules:
  0.0 342.7 jit_solution(11571263131541725120)
XLA Ops:
  0.6 0.0 copy-start
  0.7 0.7 convert_element_type.21
  1.3 0.1 pad.4.clone
  1.4 0.1 multiply_cosine_fusion
  1.5 0.1 pad_maximum_fusion
  1.6 1.3 reshape.47.gain_ref
  2.9 0.0 copy-done
  2.9 0.6 constant_dynamic-slice_fusion.1.segr_ref
  3.5 1.3 multiply_reduce_fusion
  4.8 0.7 add.10
  5.5 0.6 reshape.49.mod_ref
  6.1 1.0 copy.22.segc_ref
  7.1 80.3 %front.1 = (bf16[1024,768]{1,0:T(8,128)(2,1)}, bf16[1024,768]{1,0:T(8,128)(2,1)}, bf16[1024,768]{1,0:T(8,128)(2,1)}, bf16[6,1024,128]{2,1,0:T(8,128)(2,1)}, bf16...) custom-call(bf16[2,512,768]{2,1,0:T(8,128)(2,1)} %tok.1, ...), custom_call_target="tpu_custom_call" | custom-call | tf_op jit(solution)/shard_map/front/pallas_call | solution.py:389
  87.4 88.3 %feed.1 = (bf16[1024,768]{1,0:T(8,128)(2,1)}, f32[1024,768]{1,0:T(8,128)}, bf16[1024,768]{1,0:T(8,128)(2,1)}, bf16[2,768,384]{2,1,0:T(8,128)(2,1)}, f32[8,768]{1...) custom-call(bf16[1024,768]{1,0:T(8,128)(2,1)} %get-tuple-element.40.x_ref, ...), custom_call_target="tpu_custom_call" | custom-call | tf_op jit(solution)/shard_map/feed/pallas_call | solution.py:575
  175.7 0.7 slice.18
  176.5 0.7 maximum_bitcast_fusion.small_ref
  177.1 145.8 %back.1 = (bf16[768,1536]{1,0:T(8,128)(2,1)}, bf16[6,256,768]{2,1,0:T(8,128)(2,1)}, bf16[768,384]{1,0:T(8,128)(2,1)}, bf16[3,768,384]{2,1,0:T(8,128)(2,1)}, bf16...) custom-call(bf16[6,1024,128]{2,1,0:T(8,128)(2,1)} %get-tuple-element.36.q_re, ...), custom_call_target="tpu_custom_call" | custom-call | tf_op jit(solution)/shard_map/back/pallas_call | solution.py:844
  322.9 1.3 slice_reduce_fusion
  324.3 0.9 slice.22
  325.2 1.6 slice_reduce_fusion.1
  326.8 1.1 fusion.3
  327.9 0.0 copy-start.4
  328.0 1.1 maximum_convert_fusion
  329.0 2.1 fusion
  331.2 2.0 convert_element_type.23
  333.2 0.8 copy-done.3
  334.0 2.8 convert_element_type.25
  336.8 0.0 copy-done.2
  336.8 2.7 bitcast_convert_fusion
  339.5 1.1 copy.31
  340.7 0.8 copy-done.5
  341.5 1.1 copy.32
  (14 shorter events, 0.1 us)
Async XLA Ops:
  0.6 2.3 copy-start
  327.9 3.2 copy-start.4
  331.2 2.8 copy-start.3
  334.0 2.8 copy-start.2
  336.8 2.7 copy-start.6
  339.5 2.0 copy-start.5
  339.5 3.1 copy-start.1
